TPU v7x, 32 devices: a whole 2x2x4 slice. The times are simulated.
32 devices in a mesh: aux: 4 (over z), orb: 8 (over y, x, core).
Axes of the slice: x: 2, y: 2, z: 4, core: 2. Of those that a mesh axis runs over, the one named last changes fastest.
Arguments:
- three_centre: bfloat16 [256, 3, 3, 16, 128, 128], P(('aux', 'orb')), may hold values from -0.59765625 to 0.59765625
- block_lists: int32 [256, 3], P(('aux', 'orb')), may hold values from 0 to 7, as said below
- occupied: bfloat16 [1024, 512], P('orb'), may hold values from -0.1796875 to 0.1796875
Outputs:
- exchange_band: float32 [8, 128, 896], P('orb', 'aux')
Inputs may be any that keep to these rules, and one draw needn't show every extreme that they name: Each row of block_lists holds 3 increasing basis blocks that lie within 4 consecutive blocks. The auxiliary blocks held at orb index o list only basis blocks from o - 4 to o + 3.
All inputs are finite; a program needn't handle non-finite values.
Results may differ from a plain program's by a relative error of at most 0.0003.
Values may be sent and summed in bfloat16 or wider, within the bound.
No kernel may reach another device: no remote copies, remote signals or barrier semaphores. Data moves between devices by JAX's collectives and lax.ppermute only.
A program may use at most 128 MiB of HBM per device.

v0:
```python
import jax
import jax.numpy as jnp
from jax import lax
from jax.sharding import PartitionSpec as P


def accumulate(three_centre, block_lists, coeff_blocks, base, count):
    block_edge = three_centre.shape[-1]
    list_span = block_lists.shape[1]
    band_width = 2 * list_span + 1

    def advance(running, inputs):
        integrals, listed = inputs
        chosen = jnp.take(coeff_blocks, listed, axis=0)
        transformed = jnp.einsum(
            "mnapq,nqi->ampi", integrals, chosen, preferred_element_type=jnp.float32
        ).astype(jnp.bfloat16)
        product = jnp.einsum(
            "ampi,anqi->mnpq", transformed, transformed, preferred_element_type=jnp.float32
        )
        row_index = jnp.broadcast_to(listed[:, None] - base, (list_span, list_span)).reshape(-1)
        offset_index = (listed[None, :] - listed[:, None] + list_span).reshape(-1)
        pieces = product.reshape(list_span * list_span, block_edge, block_edge)
        return (running.at[row_index, :, offset_index, :].add(pieces), None)

    zeroed = jnp.zeros((count, block_edge, band_width, block_edge), jnp.float32)
    running, unused = lax.scan(advance, zeroed, (three_centre, block_lists))
    return running.reshape(count, block_edge, band_width * block_edge)


def per_device(three_centre, block_lists, occupied):
    full_coeffs = lax.all_gather(occupied, "orb", axis=0, tiled=True)
    block_edge = three_centre.shape[-1]
    occ_width = occupied.shape[1]
    block_count = full_coeffs.shape[0] // block_edge
    coeff_blocks = full_coeffs.reshape(block_count, block_edge, occ_width)
    summed = accumulate(three_centre, block_lists, coeff_blocks, 0, block_count)
    grouped = lax.psum_scatter(summed, "aux", scatter_dimension=1, tiled=True)
    result = lax.psum_scatter(grouped, "orb", scatter_dimension=0, tiled=True)
    return result


def solution(mesh):
    return jax.shard_map(
        per_device,
        mesh=mesh,
        in_specs=(
            P(("aux", "orb"), None, None, None, None, None),
            P(("aux", "orb"), None),
            P("orb", None),
        ),
        out_specs=P("orb", "aux", None),
        check_vma=False,
    )
```

profile of v0, /device:TPU:0, one launch (start us, length us, event | category | flops | bytes accessed | tf_op | source)
XLA Modules:
  0.0 308.1 jit_solution(6104490146273186403)
XLA Ops:
  8.1 27.4 %all-gather.2.cloned.1.call-done = bf16[1024,512]{1,0:T(8,128)(2,1)} async-done(((bf16[128,512]{1,0:T(8,128)(2,1)}), bf16[1024,512]{1,0:T(8,128)(2,1)}) %all-gather.2.cloned.1.call-update) | async-done | bytes 1048592 | tf_op jit(solution)/shard_map/all_gather | solution.py:32
  35.5 2.3 broadcast_in_dim.37
  37.8 146.3 %while.12 = (s32[]{:T(128)}, f32[8,128,7,128]{3,1,2,0:T(8,128)}, s32[8,3]{1,0:T(8,128)S(1)}, bf16[8,128,512]{2,1,0:T(8,128)(2,1)}, bf16[8,3,3,16,128,128]{5,4,3,2,1,0:T(8,128)(2,1)}, /*index=5*/s32[]{:T(128)}) while((s32[]{:T(128)}, f32[8,128,7,128]{3,1,2,0:T(8,128)}, s32[8,3]{1,0:T(8,128)S(1)}, bf16[8,128,512]{2,1,0:T(8,128)(2,1)}, ...), condition=%wide.region_2.3_spmd, body=%wide.region_0.2_spmd.sunk | while | flops 7254590464 | bytes 14555716 | solution.py:27
  39.9 12.8 %fusion.43 = f32[3,3,128,128]{2,3,0,1:T(8,128)S(1)} fusion(bf16[3,128,512]{2,1,0:T(8,128)(2,1)S(1)} %gather_fusion, pred[3]{0:T(512)(128)(4,1)S(1)} %get-tuple-element.137, bf16[8,3,3,16,128,128]{5,4,3,2,1,0:T(8,128)(2,1)} %get-tuple-element.154, s32[]{:T(128)S(6)} %copy.55), kind=kOutput, calls=%fused_computation.8.clone.1 | convolution fusion | flops 7254441984 | bytes 10815488 | tf_op jit(solution)/shard_map/while/body/eval_jaxpr/ampi,anqi->mnpq/dot_general | solution.py:18
  52.9 3.2 %scatter_fusion = f32[8,128,7,128]{3,1,2,0:T(8,128)} fusion(f32[8,128,7,128]{3,1,2,0:T(8,128)} %get-tuple-element.145, s32[9]{0:T(128)S(1)} %fusion.41, f32[9,128,128]{2,1,0:T(8,128)S(1)} %bitcast.83), kind=kCustom, calls=%fused_computation.1.clone.1 | custom fusion | flops 147456 | bytes 1769544 | tf_op jit(solution)/shard_map/while/body/eval_jaxpr/scatter-add | solution.py:24
  58.2 12.8 %fusion.43 = f32[3,3,128,128]{2,3,0,1:T(8,128)S(1)} fusion(bf16[3,128,512]{2,1,0:T(8,128)(2,1)S(1)} %gather_fusion, pred[3]{0:T(512)(128)(4,1)S(1)} %get-tuple-element.137, bf16[8,3,3,16,128,128]{5,4,3,2,1,0:T(8,128)(2,1)} %get-tuple-element.154, s32[]{:T(128)S(6)} %copy.55), kind=kOutput, calls=%fused_computation.8.clone.1 | convolution fusion | flops 7254441984 | bytes 10815488 | tf_op jit(solution)/shard_map/while/body/eval_jaxpr/ampi,anqi->mnpq/dot_general | solution.py:18
  71.3 3.1 %scatter_fusion = f32[8,128,7,128]{3,1,2,0:T(8,128)} fusion(f32[8,128,7,128]{3,1,2,0:T(8,128)} %get-tuple-element.145, s32[9]{0:T(128)S(1)} %fusion.41, f32[9,128,128]{2,1,0:T(8,128)S(1)} %bitcast.83), kind=kCustom, calls=%fused_computation.1.clone.1 | custom fusion | flops 147456 | bytes 1769544 | tf_op jit(solution)/shard_map/while/body/eval_jaxpr/scatter-add | solution.py:24
  76.5 12.8 %fusion.43 = f32[3,3,128,128]{2,3,0,1:T(8,128)S(1)} fusion(bf16[3,128,512]{2,1,0:T(8,128)(2,1)S(1)} %gather_fusion, pred[3]{0:T(512)(128)(4,1)S(1)} %get-tuple-element.137, bf16[8,3,3,16,128,128]{5,4,3,2,1,0:T(8,128)(2,1)} %get-tuple-element.154, s32[]{:T(128)S(6)} %copy.55), kind=kOutput, calls=%fused_computation.8.clone.1 | convolution fusion | flops 7254441984 | bytes 10815488 | tf_op jit(solution)/shard_map/while/body/eval_jaxpr/ampi,anqi->mnpq/dot_general | solution.py:18
  89.6 3.0 scatter_fusion
  94.7 12.8 %fusion.43 = f32[3,3,128,128]{2,3,0,1:T(8,128)S(1)} fusion(bf16[3,128,512]{2,1,0:T(8,128)(2,1)S(1)} %gather_fusion, pred[3]{0:T(512)(128)(4,1)S(1)} %get-tuple-element.137, bf16[8,3,3,16,128,128]{5,4,3,2,1,0:T(8,128)(2,1)} %get-tuple-element.154, s32[]{:T(128)S(6)} %copy.55), kind=kOutput, calls=%fused_computation.8.clone.1 | convolution fusion | flops 7254441984 | bytes 10815488 | tf_op jit(solution)/shard_map/while/body/eval_jaxpr/ampi,anqi->mnpq/dot_general | solution.py:18
  107.8 3.1 %scatter_fusion = f32[8,128,7,128]{3,1,2,0:T(8,128)} fusion(f32[8,128,7,128]{3,1,2,0:T(8,128)} %get-tuple-element.145, s32[9]{0:T(128)S(1)} %fusion.41, f32[9,128,128]{2,1,0:T(8,128)S(1)} %bitcast.83), kind=kCustom, calls=%fused_computation.1.clone.1 | custom fusion | flops 147456 | bytes 1769544 | tf_op jit(solution)/shard_map/while/body/eval_jaxpr/scatter-add | solution.py:24
  113.1 12.8 %fusion.43 = f32[3,3,128,128]{2,3,0,1:T(8,128)S(1)} fusion(bf16[3,128,512]{2,1,0:T(8,128)(2,1)S(1)} %gather_fusion, pred[3]{0:T(512)(128)(4,1)S(1)} %get-tuple-element.137, bf16[8,3,3,16,128,128]{5,4,3,2,1,0:T(8,128)(2,1)} %get-tuple-element.154, s32[]{:T(128)S(6)} %copy.55), kind=kOutput, calls=%fused_computation.8.clone.1 | convolution fusion | flops 7254441984 | bytes 10815488 | tf_op jit(solution)/shard_map/while/body/eval_jaxpr/ampi,anqi->mnpq/dot_general | solution.py:18
  126.1 3.1 %scatter_fusion = f32[8,128,7,128]{3,1,2,0:T(8,128)} fusion(f32[8,128,7,128]{3,1,2,0:T(8,128)} %get-tuple-element.145, s32[9]{0:T(128)S(1)} %fusion.41, f32[9,128,128]{2,1,0:T(8,128)S(1)} %bitcast.83), kind=kCustom, calls=%fused_computation.1.clone.1 | custom fusion | flops 147456 | bytes 1769544 | tf_op jit(solution)/shard_map/while/body/eval_jaxpr/scatter-add | solution.py:24
  131.3 12.8 %fusion.43 = f32[3,3,128,128]{2,3,0,1:T(8,128)S(1)} fusion(bf16[3,128,512]{2,1,0:T(8,128)(2,1)S(1)} %gather_fusion, pred[3]{0:T(512)(128)(4,1)S(1)} %get-tuple-element.137, bf16[8,3,3,16,128,128]{5,4,3,2,1,0:T(8,128)(2,1)} %get-tuple-element.154, s32[]{:T(128)S(6)} %copy.55), kind=kOutput, calls=%fused_computation.8.clone.1 | convolution fusion | flops 7254441984 | bytes 10815488 | tf_op jit(solution)/shard_map/while/body/eval_jaxpr/ampi,anqi->mnpq/dot_general | solution.py:18
  144.4 3.1 %scatter_fusion = f32[8,128,7,128]{3,1,2,0:T(8,128)} fusion(f32[8,128,7,128]{3,1,2,0:T(8,128)} %get-tuple-element.145, s32[9]{0:T(128)S(1)} %fusion.41, f32[9,128,128]{2,1,0:T(8,128)S(1)} %bitcast.83), kind=kCustom, calls=%fused_computation.1.clone.1 | custom fusion | flops 147456 | bytes 1769544 | tf_op jit(solution)/shard_map/while/body/eval_jaxpr/scatter-add | solution.py:24
  149.6 12.8 %fusion.43 = f32[3,3,128,128]{2,3,0,1:T(8,128)S(1)} fusion(bf16[3,128,512]{2,1,0:T(8,128)(2,1)S(1)} %gather_fusion, pred[3]{0:T(512)(128)(4,1)S(1)} %get-tuple-element.137, bf16[8,3,3,16,128,128]{5,4,3,2,1,0:T(8,128)(2,1)} %get-tuple-element.154, s32[]{:T(128)S(6)} %copy.55), kind=kOutput, calls=%fused_computation.8.clone.1 | convolution fusion | flops 7254441984 | bytes 10815488 | tf_op jit(solution)/shard_map/while/body/eval_jaxpr/ampi,anqi->mnpq/dot_general | solution.py:18
  162.7 3.1 %scatter_fusion = f32[8,128,7,128]{3,1,2,0:T(8,128)} fusion(f32[8,128,7,128]{3,1,2,0:T(8,128)} %get-tuple-element.145, s32[9]{0:T(128)S(1)} %fusion.41, f32[9,128,128]{2,1,0:T(8,128)S(1)} %bitcast.83), kind=kCustom, calls=%fused_computation.1.clone.1 | custom fusion | flops 147456 | bytes 1769544 | tf_op jit(solution)/shard_map/while/body/eval_jaxpr/scatter-add | solution.py:24
  167.9 12.8 %fusion.43 = f32[3,3,128,128]{2,3,0,1:T(8,128)S(1)} fusion(bf16[3,128,512]{2,1,0:T(8,128)(2,1)S(1)} %gather_fusion, pred[3]{0:T(512)(128)(4,1)S(1)} %get-tuple-element.137, bf16[8,3,3,16,128,128]{5,4,3,2,1,0:T(8,128)(2,1)} %get-tuple-element.154, s32[]{:T(128)S(6)} %copy.55), kind=kOutput, calls=%fused_computation.8.clone.1 | convolution fusion | flops 7254441984 | bytes 10815488 | tf_op jit(solution)/shard_map/while/body/eval_jaxpr/ampi,anqi->mnpq/dot_general | solution.py:18
  181.0 3.1 %scatter_fusion = f32[8,128,7,128]{3,1,2,0:T(8,128)} fusion(f32[8,128,7,128]{3,1,2,0:T(8,128)} %get-tuple-element.145, s32[9]{0:T(128)S(1)} %fusion.41, f32[9,128,128]{2,1,0:T(8,128)S(1)} %bitcast.83), kind=kCustom, calls=%fused_computation.1.clone.1 | custom fusion | flops 147456 | bytes 1769544 | tf_op jit(solution)/shard_map/while/body/eval_jaxpr/scatter-add | solution.py:24
  184.1 5.0 %copy.25 = f32[8,128,7,128]{1,3,2,0:T(8,128)} copy(f32[8,128,7,128]{3,1,2,0:T(8,128)} %get-tuple-element.70) | data formatting | bytes 7340032 | tf_op jit(solution)/shard_map/while | solution.py:27
  189.1 4.7 %copy.26 = f32[8,128,896]{2,0,1:T(8,128)} copy(f32[8,128,896]{1,2,0:T(8,128)} %bitcast.84) | data formatting | bytes 7340032 | tf_op jit(solution)/shard_map/reshape | solution.py:28
  193.9 68.6 %reduce-scatter.3.cloned.1.call-done = f32[8,32,896]{2,0,1:T(8,128)} async-done(((f32[8,128,896]{2,0,1:T(8,128)}), f32[8,32,896]{2,0,1:T(8,128)}) %reduce-scatter.3.cloned.1.call-update) | async-done | bytes 917520 | tf_op jit(solution)/shard_map/reduce_scatter | solution.py:38
  262.5 2.3 copy.27
  264.9 36.7 %reduce-scatter.5.cloned.1.call-done = f32[1,32,896]{2,1,0:T(8,128)} async-done(((f32[8,32,896]{2,1,0:T(8,128)}), f32[1,32,896]{2,1,0:T(8,128)}) %reduce-scatter.5.cloned.1.call-update) | async-done | bytes 114704 | tf_op jit(solution)/shard_map/reduce_scatter | solution.py:39
  (87 shorter events, 20.0 us)
Async XLA Ops:
  6.5 28.9 %all-gather.2.cloned.1.call-start = ((), (), s32[]{:S(2)}) async-start(), calls=%async_computation.2 | async-start | bytes 1179648 | tf_op jit(solution)/shard_map/all_gather | solution.py:32
  7.3 255.3 %reduce-scatter.3.cloned.1.call-start = ((), (), s32[]{:S(2)}) async-start(), calls=%async_computation.3 | async-start | bytes 4587520 | tf_op jit(solution)/shard_map/reduce_scatter | solution.py:38
  193.9 107.7 %reduce-scatter.5.cloned.1.call-start = ((), (), s32[]{:S(2)}) async-start(), calls=%async_computation.4 | async-start | bytes 1032192 | tf_op jit(solution)/shard_map/reduce_scatter | solution.py:39
Sparse Core Ops, SparseCore 0:
  9.2 26.1 all-gather.1
  194.0 68.4 reduce-scatter.2
  265.7 35.8 reduce-scatter.4
where the time goes:
time: 309 us; the launch traced here: 308 us
  waiting for transfers between devices  133 us (43%)
  matrix products  103 us (33%)
  local copies, waits for them, and re-layouts  33.2 us (11%)
  other arithmetic  25.3 us (8%)
  between operations  13.1 us (4%)
    dot_general x8, matrix products, advance(): jnp.einsum('ampi,anqi->mnpq', transformed, transformed, preferred_element...  103 us
    reduce_scatter x1, waiting for transfers between devices, per_device(): grouped = lax.psum_scatter(summed, 'aux', scatter_dimension=1, tiled=True)  68.6 us
    reduce_scatter x1, waiting for transfers between devices, per_device(): result = lax.psum_scatter(grouped, 'orb', scatter_dimension=0, tiled=True)  36.7 us
    all_gather x1, waiting for transfers between devices, per_device(): full_coeffs = lax.all_gather(occupied, 'orb', axis=0, tiled=True)  27.4 us
    scatter-add x8, other arithmetic, advance(): return (running.at[row_index, :, offset_index, :].add(pieces), None)  25 us
    gather x8, local copies, waits for them, and re-layouts, advance(): chosen = jnp.take(coeff_blocks, listed, axis=0)  14.4 us
  transfers between devices with their start and end apart: 3, of which 3 were waited for; matrix products, arithmetic and copies ran while one was open for 0% of the time, Pallas kernels for 0%

commit v1 on v0

v1 whole, which is shorter than its diff:
```python
import functools

import jax
import jax.numpy as jnp
from jax import lax
from jax.experimental import pallas as pl
from jax.experimental.pallas import tpu as pltpu
from jax.sharding import PartitionSpec as P

ROWS_BY_ROWS = (((1,), (1,)), ((), ()))


def contract_rows(left, right):
    return lax.dot_general(left, right, ROWS_BY_ROWS, preferred_element_type=jnp.float32)


def band_kernel(sizes, place_ref, lists_ref, *refs):
    aux_blocks, span, depth, edge, width, slots, groups = sizes
    coeff_refs, refs = refs[:slots], refs[slots:]
    integrals_ref, keep_ref, send_ref = refs[:3]
    coeffs, chosen, integrals, half, total, band, load_sem, coeff_sem, out_sem = refs[3:]
    orb, aux = place_ref[0], place_ref[1]
    rows = edge // groups

    def load(block, m):
        return pltpu.make_async_copy(integrals_ref.at[block, m], integrals.at[m], load_sem.at[m])

    coeff_loads = [pltpu.make_async_copy(coeff_refs[s], coeffs.at[s], coeff_sem.at[s]) for s in range(slots)]
    for copy in coeff_loads:
        copy.start()
    for m in range(span):
        load(0, m).start()
    band[...] = jnp.zeros_like(band)
    for copy in coeff_loads:
        copy.wait()

    def step(block, carry):
        listed = [lists_ref[block, j] for j in range(span)]
        for n in range(span):
            chosen[n * edge : (n + 1) * edge, :] = coeffs[listed[n] ^ orb]
        for m in range(span):
            load(block, m).wait()
            left = jnp.concatenate([integrals[m, n].reshape(depth * edge, edge) for n in range(span)], axis=1)
            made = jnp.dot(left, chosen[...], preferred_element_type=jnp.float32).astype(jnp.bfloat16)
            for a in range(depth):
                half[m * edge : (m + 1) * edge, a * width : (a + 1) * width] = made[a * edge : (a + 1) * edge]

            @pl.when(block + 1 < aux_blocks)
            def _():
                load(block + 1, m).start()

        last = (span - 1) * edge
        total[:, :last] = contract_rows(half[...], half[:last])
        total[last:, last:] = contract_rows(half[last:], half[last:])
        for m in range(span):
            for n in range(m + 1):
                piece = total[m * edge : (m + 1) * edge, n * edge : (n + 1) * edge]
                pairs = [(m, n, piece)] if m == n else [(m, n, piece), (n, m, piece.T)]
                for j, k, value in pairs:
                    slot = listed[j] ^ orb
                    offset = listed[k] - listed[j] + span
                    for g in range(groups):
                        place = (slot & 1, slot >> 1, g ^ aux, offset)
                        band[place] += value[g * rows : (g + 1) * rows]
        return carry

    lax.fori_loop(0, aux_blocks, step, 0)
    outs = [pltpu.make_async_copy(band.at[i], ref, out_sem.at[i]) for i, ref in enumerate((keep_ref, send_ref))]
    for copy in outs:
        copy.start()
    for copy in outs:
        copy.wait()


def band_partials(place, block_lists, coeff_slots, three_centre, groups):
    aux_blocks, span, _, depth, edge, _ = three_centre.shape
    width = coeff_slots[0].shape[1]
    slots = len(coeff_slots)
    offsets = 2 * span + 1
    sizes = (aux_blocks, span, depth, edge, width, slots, groups)
    part = (slots // 2, groups, offsets, edge // groups, edge)
    anywhere = pl.BlockSpec(memory_space=pl.ANY)
    scalars = pl.BlockSpec(memory_space=pltpu.SMEM)
    return pl.pallas_call(
        functools.partial(band_kernel, sizes),
        out_shape=[jax.ShapeDtypeStruct(part, jnp.float32)] * 2,
        in_specs=[scalars, scalars] + [anywhere] * (slots + 1),
        out_specs=[anywhere] * 2,
        scratch_shapes=[
            pltpu.VMEM((slots, edge, width), jnp.bfloat16),
            pltpu.VMEM((span * edge, width), jnp.bfloat16),
            pltpu.VMEM((span, span, depth, edge, edge), jnp.bfloat16),
            pltpu.VMEM((span * edge, depth * width), jnp.bfloat16),
            pltpu.VMEM((span * edge, span * edge), jnp.float32),
            pltpu.VMEM((2,) + part, jnp.float32),
            pltpu.SemaphoreType.DMA((span,)),
            pltpu.SemaphoreType.DMA((slots,)),
            pltpu.SemaphoreType.DMA((2,)),
        ],
        compiler_params=pltpu.CompilerParams(vmem_limit_bytes=56 * 2**20),
        name="band_partials",
    )(place, block_lists, *coeff_slots, three_centre)


def per_device(orb_size, aux_size, three_centre, block_lists, occupied):
    def swap(value, axis, bits):
        size = {"orb": orb_size, "aux": aux_size}[axis]
        return lax.ppermute(value, axis, [(i, i ^ bits) for i in range(size)])

    place = jnp.stack([lax.axis_index("orb"), lax.axis_index("aux")]).astype(jnp.int32)
    slots = {0: occupied, 1: swap(occupied, "orb", 1)}
    for s in range(2, orb_size, 2):
        slots[s] = swap(occupied, "orb", s)
    for s in range(2, orb_size, 2):
        slots[s + 1] = swap(slots[s], "orb", 1)
    keep, send = band_partials(place, block_lists, [slots[s] for s in range(orb_size)], three_centre, aux_size)

    summed = keep + swap(send, "orb", 1)
    bits = list(range(1, orb_size.bit_length() - 1))
    halves = []
    for part in range(2):
        taken = summed[:, part * (aux_size // 2) : (part + 1) * (aux_size // 2)]
        taken = taken.reshape((2,) * len(bits) + taken.shape[1:])
        left = bits[::-1]
        for bit in bits if part == 0 else left[:]:
            axis = left.index(bit)
            kept = lax.index_in_dim(taken, 0, axis, keepdims=False)
            taken = kept + swap(lax.index_in_dim(taken, 1, axis, keepdims=False), "orb", 1 << bit)
            left.remove(bit)
        halves.append(taken)
    rows = jnp.concatenate(halves, axis=0)
    step = 1
    while step < aux_size:
        rows = rows[0::2] + swap(rows[1::2], "aux", step)
        step *= 2
    return jnp.transpose(rows, (0, 2, 1, 3)).reshape(1, rows.shape[2], rows.shape[1] * rows.shape[3])


def solution(mesh):
    return jax.shard_map(
        functools.partial(per_device, mesh.shape["orb"], mesh.shape["aux"]),
        mesh=mesh,
        in_specs=(
            P(("aux", "orb"), None, None, None, None, None),
            P(("aux", "orb"), None),
            P("orb", None),
        ),
        out_specs=P("orb", "aux", None),
        check_vma=False,
    )
```

time: 309 us -> 127 us (0.41)
  matrix products: 103 us -> 0 us
  waiting for transfers between devices: 133 us -> 33.3 us
  Pallas kernels: 0 us -> 70.8 us
  local copies, waits for them, and re-layouts: 33.2 us -> 2.89 us
  other arithmetic: 25.3 us -> 3.45 us
  starting transfers between devices: 0.08 us -> 16 us
  between operations: 13.1 us -> 0.16 us
    reduce_scatter x2 -> x0, waiting for transfers between devices: 105 us -> none  [the longest x1 68.6 us: per_device(): grouped = lax.psum_scatter(summed, 'aux', scatter_dimension=1, tiled=True)]
    dot_general x8 -> x0, matrix products: 103 us -> none  [advance(): jnp.einsum('ampi,anqi->mnpq', transformed, transformed, preferred_element...]
    pallas_call x0 -> x1, Pallas kernels: none -> 70.8 us  [band_partials(): pl.pallas_call(functools.partial(band_kernel, sizes), out_shape=[jax.Shap...]
    ppermute x0 -> x14, waiting for transfers between devices: none -> 33.3 us  [swap(): return lax.ppermute(value, axis, [(i, i ^ bits) for i in range(size)])]
    all_gather x1 -> x0, waiting for transfers between devices: 27.4 us -> none  [per_device(): full_coeffs = lax.all_gather(occupied, 'orb', axis=0, tiled=True)]
    scatter-add x8 -> x0, other arithmetic: 25 us -> none  [advance(): return (running.at[row_index, :, offset_index, :].add(pieces), None)]
    ppermute x0 -> x14, starting transfers between devices: none -> 16 us  [swap(): return lax.ppermute(value, axis, [(i, i ^ bits) for i in range(size)])]
    gather x8 -> x0, local copies, waits for them, and re-layouts: 14.4 us -> none  [advance(): chosen = jnp.take(coeff_blocks, listed, axis=0)]
  transfers between devices with their start and end apart: 3 -> 14, of which waited for: 3 -> 9; matrix products, arithmetic and copies ran while one was open for 0% -> 2% of each run, Pallas kernels for 0% -> 0%
where the time goes in v1:
time: 127 us
  Pallas kernels  70.8 us (56%)
  waiting for transfers between devices  33.3 us (26%)
  starting transfers between devices  16 us (13%)
  other arithmetic  3.45 us (3%)
  local copies, waits for them, and re-layouts  2.89 us (2%)
    pallas_call x1, Pallas kernels, band_partials(): pl.pallas_call(functools.partial(band_kernel, sizes), out_shape=[jax.Shap...  70.8 us
    ppermute x14, waiting for transfers between devices, swap(): return lax.ppermute(value, axis, [(i, i ^ bits) for i in range(size)])  33.3 us
    ppermute x14, starting transfers between devices, swap(): return lax.ppermute(value, axis, [(i, i ^ bits) for i in range(size)])  16 us
    unnamed x15, local copies, waits for them, and re-layouts  2.7 us
  transfers between devices with their start and end apart: 14, of which 9 were waited for; matrix products, arithmetic and copies ran while one was open for 2% of the time, Pallas kernels for 0%

profile of v1, /device:TPU:0, one launch (start us, length us, event | category | flops | bytes accessed | tf_op | source)
XLA Modules:
  0.0 126.7 jit_solution(5896501936752345568)
XLA Ops:
  0.0 3.0 %collective-permute-start.3 = (bf16[128,512]{1,0:T(8,128)(2,1)}, bf16[128,512]{1,0:T(8,128)(2,1)S(1)}, u32[]{:S(2)}, u32[]{:S(2)}) collective-permute-start(bf16[128,512]{1,0:T(8,128)(2,1)} %refs_0_.1), channel_id=1, source_target_pairs={{0,4},{1,5},{2,6},{3,7},{4,0},{5,1},{6,2},{7,3},{8,12},{9,13},{10,... | collective-permute-start | bytes 393224 | tf_op jit(solution)/shard_map/ppermute | solution.py:108
  3.0 1.5 %collective-permute-start.1 = (bf16[128,512]{1,0:T(8,128)(2,1)}, bf16[128,512]{1,0:T(8,128)(2,1)S(1)}, u32[]{:S(2)}, u32[]{:S(2)}) collective-permute-start(bf16[128,512]{1,0:T(8,128)(2,1)} %refs_0_.1), channel_id=1, source_target_pairs={{0,2},{1,3},{2,0},{3,1},{4,6},{5,7},{6,4},{7,5},{8,10},{9,11},{10,... | collective-permute-start | bytes 393224 | tf_op jit(solution)/shard_map/ppermute | solution.py:108
  4.5 2.2 %collective-permute-done.3.refs_4_ = bf16[128,512]{1,0:T(8,128)(2,1)S(1)} collective-permute-done((bf16[128,512]{1,0:T(8,128)(2,1)}, bf16[128,512]{1,0:T(8,128)(2,1)S(1)}, u32[]{:S(2)}, u32[]{:S(2)}) %collective-permute-start.3) | collective-permute-done | bytes 131104 | tf_op jit(solution)/shard_map/ppermute | solution.py:108
  6.7 2.9 %collective-permute-done.1.refs_2_ = bf16[128,512]{1,0:T(8,128)(2,1)S(1)} collective-permute-done((bf16[128,512]{1,0:T(8,128)(2,1)}, bf16[128,512]{1,0:T(8,128)(2,1)S(1)}, u32[]{:S(2)}, u32[]{:S(2)}) %collective-permute-start.1) | collective-permute-done | bytes 131104 | tf_op jit(solution)/shard_map/ppermute | solution.py:108
  9.5 1.1 collective-permute-done.5.refs_6_
  10.7 1.4 %copy.5.lists_ref = s32[8,3]{1,0:T(8,128)} copy(s32[8,3]{0,1:T(4,128)} %param.4) | data formatting | bytes 192 | tf_op args[1]
  12.0 0.6 pad_add_fusion.place_ref
  12.7 0.6 copy-done.3
  13.4 0.6 copy-done.6
  14.1 70.8 %band_partials.1 = (f32[4,4,7,32,128]{4,3,2,1,0:T(8,128)}, f32[4,4,7,32,128]{4,3,2,1,0:T(8,128)}) custom-call(s32[2]{0:T(128)} %pad_add_fusion.place_ref, s32[8,3]{1,0:T(8,128)} %copy.5.lists_ref, bf16[128,512]{1,0:T(8,128)(2,1)} %refs_0_.1, bf16[128,512]{1,0:T(8,128)(2,1)} %copy-done.3, bf16[128,512]{1,0:T(8,128)(2,1)} %copy-done.1, ...), custom_call_target="tpu_custom_call" | custom-call | tf_op jit(solution)/shard_map/band_partials/pallas_call | solution.py:84
  85.4 3.6 %collective-permute-done.7 = f32[4,4,7,32,128]{4,3,2,1,0:T(8,128)S(1)} collective-permute-done((f32[4,4,7,32,128]{4,3,2,1,0:T(8,128)}, f32[4,4,7,32,128]{4,3,2,1,0:T(8,128)S(1)}, u32[]{:S(2)}, u32[]{:S(2)}) %collective-permute-start.7) | collective-permute-done | bytes 1835040 | tf_op jit(solution)/shard_map/ppermute | solution.py:108
  89.0 1.9 %add.21 = f32[4,4,7,32,128]{4,3,2,1,0:T(8,128)S(1)} add(f32[4,4,7,32,128]{4,3,2,1,0:T(8,128)} %get-tuple-element.7, f32[4,4,7,32,128]{4,3,2,1,0:T(8,128)S(1)} %collective-permute-done.7) | non-fusion elementwise | flops 458752 | bytes 5505024 | tf_op jit(solution)/shard_map/add | solution.py:118
  91.0 1.9 %collective-permute-start.10 = (f32[2,2,7,32,128]{4,3,2,1,0:T(8,128)S(1)}, f32[2,2,7,32,128]{4,3,2,1,0:T(8,128)S(1)}, u32[]{:S(2)}, u32[]{:S(2)}) collective-permute-start(f32[2,2,7,32,128]{4,3,2,1,0:T(8,128)S(1)} %slice.65), channel_id=1, source_target_pairs={{0,4},{1,5},{2,6},{3,7},{4,0},{5,1},{6,2},{7,3},{8,12},{9,13},{10,... | collective-permute-start | bytes 1376264 | tf_op jit(solution)/shard_map/ppermute | solution.py:108
  93.0 1.4 %collective-permute-start.8 = (f32[2,2,7,32,128]{4,3,2,1,0:T(8,128)S(1)}, f32[2,2,7,32,128]{4,3,2,1,0:T(8,128)S(1)}, u32[]{:S(2)}, u32[]{:S(2)}) collective-permute-start(f32[2,2,7,32,128]{4,3,2,1,0:T(8,128)S(1)} %slice_bitcast_fusion), channel_id=1, source_target_pairs={{0,2},{1,3},{2,0},{3,1},{4,6},{5,7},{6,4},{7,5},{8,10},{9,11},{10,... | collective-permute-start | bytes 1376264 | tf_op jit(solution)/shard_map/ppermute | solution.py:108
  94.5 9.5 %collective-permute-done.10 = f32[2,2,7,32,128]{4,3,2,1,0:T(8,128)S(1)} collective-permute-done((f32[2,2,7,32,128]{4,3,2,1,0:T(8,128)S(1)}, f32[2,2,7,32,128]{4,3,2,1,0:T(8,128)S(1)}, u32[]{:S(2)}, u32[]{:S(2)}) %collective-permute-start.10) | collective-permute-done | bytes 458784 | tf_op jit(solution)/shard_map/ppermute | solution.py:108
  104.1 1.8 %collective-permute-start.11 = (f32[2,7,32,128]{3,2,1,0:T(8,128)S(1)}, f32[2,7,32,128]{3,2,1,0:T(8,128)S(1)}, u32[]{:S(2)}, u32[]{:S(2)}) collective-permute-start(f32[2,7,32,128]{3,2,1,0:T(8,128)S(1)} %slice_bitcast_fusion.2), channel_id=1, source_target_pairs={{0,2},{1,3},{2,0},{3,1},{4,6},{5,7},{6,4},{7,5},{8,10},{9,11},{10,... | collective-permute-start | bytes 688136 | tf_op jit(solution)/shard_map/ppermute | solution.py:108
  106.0 1.5 %collective-permute-start.9 = (f32[2,7,32,128]{3,2,1,0:T(8,128)S(1)}, f32[2,7,32,128]{3,2,1,0:T(8,128)S(1)}, u32[]{:S(2)}, u32[]{:S(2)}) collective-permute-start(f32[2,7,32,128]{3,2,1,0:T(8,128)S(1)} %slice_bitcast_fusion.4), channel_id=1, source_target_pairs={{0,4},{1,5},{2,6},{3,7},{4,0},{5,1},{6,2},{7,3},{8,12},{9,13},{10,... | collective-permute-start | bytes 688136 | tf_op jit(solution)/shard_map/ppermute | solution.py:108
  107.4 4.0 %collective-permute-done.11 = f32[2,7,32,128]{3,2,1,0:T(8,128)S(1)} collective-permute-done((f32[2,7,32,128]{3,2,1,0:T(8,128)S(1)}, f32[2,7,32,128]{3,2,1,0:T(8,128)S(1)}, u32[]{:S(2)}, u32[]{:S(2)}) %collective-permute-start.11) | collective-permute-done | bytes 229408 | tf_op jit(solution)/shard_map/ppermute | solution.py:108
  111.4 1.4 %collective-permute-done.9 = f32[2,7,32,128]{3,2,1,0:T(8,128)S(1)} collective-permute-done((f32[2,7,32,128]{3,2,1,0:T(8,128)S(1)}, f32[2,7,32,128]{3,2,1,0:T(8,128)S(1)}, u32[]{:S(2)}, u32[]{:S(2)}) %collective-permute-start.9) | collective-permute-done | bytes 229408 | tf_op jit(solution)/shard_map/ppermute | solution.py:108
  112.9 1.5 %collective-permute-start.12 = (f32[2,7,32,128]{3,2,1,0:T(8,128)S(1)}, f32[2,7,32,128]{3,2,1,0:T(8,128)S(1)}, u32[]{:S(2)}, u32[]{:S(2)}) collective-permute-start(f32[2,7,32,128]{3,2,1,0:T(8,128)S(1)} %slice.56), channel_id=1, source_target_pairs={{0,8},{8,0},{16,24},{24,16},{1,9},{9,1},{17,25},{25,17},{2,10},{10... | collective-permute-start | bytes 688136 | tf_op jit(solution)/shard_map/ppermute | solution.py:108
  114.4 4.6 %collective-permute-done.12 = f32[2,7,32,128]{3,2,1,0:T(8,128)S(1)} collective-permute-done((f32[2,7,32,128]{3,2,1,0:T(8,128)S(1)}, f32[2,7,32,128]{3,2,1,0:T(8,128)S(1)}, u32[]{:S(2)}, u32[]{:S(2)}) %collective-permute-start.12) | collective-permute-done | bytes 229408 | tf_op jit(solution)/shard_map/ppermute | solution.py:108
  119.1 2.9 %collective-permute-start.13 = (f32[1,7,32,128]{3,2,1,0:T(8,128)S(1)}, f32[1,7,32,128]{3,2,1,0:T(8,128)S(1)}, u32[]{:S(2)}, u32[]{:S(2)}) collective-permute-start(f32[1,7,32,128]{3,2,1,0:T(8,128)S(1)} %slice.69), channel_id=1, source_target_pairs={{0,16},{8,24},{16,0},{24,8},{1,17},{9,25},{17,1},{25,9},{2,18},{10... | collective-permute-start | bytes 344072 | tf_op jit(solution)/shard_map/ppermute | solution.py:108
  122.0 4.1 %collective-permute-done.13 = f32[1,7,32,128]{3,2,1,0:T(8,128)S(1)} collective-permute-done((f32[1,7,32,128]{3,2,1,0:T(8,128)S(1)}, f32[1,7,32,128]{3,2,1,0:T(8,128)S(1)}, u32[]{:S(2)}, u32[]{:S(2)}) %collective-permute-start.13) | collective-permute-done | bytes 114720 | tf_op jit(solution)/shard_map/ppermute | solution.py:108
  126.0 0.7 copy_bitcast_fusion
  (36 shorter events, 1.2 us)
Async XLA Ops:
  0.0 6.7 %collective-permute-start.3 = (bf16[128,512]{1,0:T(8,128)(2,1)}, bf16[128,512]{1,0:T(8,128)(2,1)S(1)}, u32[]{:S(2)}, u32[]{:S(2)}) collective-permute-start(bf16[128,512]{1,0:T(8,128)(2,1)} %refs_0_.1), channel_id=1, source_target_pairs={{0,4},{1,5},{2,6},{3,7},{4,0},{5,1},{6,2},{7,3},{8,12},{9,13},{10,... | collective-permute-start | bytes 393224 | tf_op jit(solution)/shard_map/ppermute | solution.py:108
  3.0 6.6 %collective-permute-start.1 = (bf16[128,512]{1,0:T(8,128)(2,1)}, bf16[128,512]{1,0:T(8,128)(2,1)S(1)}, u32[]{:S(2)}, u32[]{:S(2)}) collective-permute-start(bf16[128,512]{1,0:T(8,128)(2,1)} %refs_0_.1), channel_id=1, source_target_pairs={{0,2},{1,3},{2,0},{3,1},{4,6},{5,7},{6,4},{7,5},{8,10},{9,11},{10,... | collective-permute-start | bytes 393224 | tf_op jit(solution)/shard_map/ppermute | solution.py:108
  4.5 6.2 %collective-permute-start.5 = (bf16[128,512]{1,0:T(8,128)(2,1)}, bf16[128,512]{1,0:T(8,128)(2,1)S(1)}, u32[]{:S(2)}, u32[]{:S(2)}) collective-permute-start(bf16[128,512]{1,0:T(8,128)(2,1)} %refs_0_.1), channel_id=1, source_target_pairs={{0,6},{1,7},{2,4},{3,5},{4,2},{5,3},{6,0},{7,1},{8,14},{9,15},{10,... | collective-permute-start | bytes 393224 | tf_op jit(solution)/shard_map/ppermute | solution.py:108
  4.5 8.2 %collective-permute-start = (bf16[128,512]{1,0:T(8,128)(2,1)}, bf16[128,512]{1,0:T(8,128)(2,1)S(1)}, u32[]{:S(2)}, u32[]{:S(2)}) collective-permute-start(bf16[128,512]{1,0:T(8,128)(2,1)} %refs_0_.1), channel_id=1, source_target_pairs={{0,1},{1,0},{2,3},{3,2},{4,5},{5,4},{6,7},{7,6},{8,9},{9,8},{10,11... | collective-permute-start | bytes 393224 | tf_op jit(solution)/shard_map/ppermute | solution.py:108
  6.7 6.0 %copy-start = (bf16[128,512]{1,0:T(8,128)(2,1)}, bf16[128,512]{1,0:T(8,128)(2,1)S(1)}, u32[]{:S(2)}) copy-start(bf16[128,512]{1,0:T(8,128)(2,1)S(1)} %collective-permute-done.3.refs_4_) | copy-start | bytes 393220
  6.7 6.0 %collective-permute-start.4 = (bf16[128,512]{1,0:T(8,128)(2,1)S(1)}, bf16[128,512]{1,0:T(8,128)(2,1)S(1)}, u32[]{:S(2)}, u32[]{:S(2)}) collective-permute-start(bf16[128,512]{1,0:T(8,128)(2,1)S(1)} %collective-permute-done.3.refs_4_), channel_id=1, source_target_pairs={{0,1},{1,0},{2,3},{3,2},{4,5},{5,4},{6,7},{7,6},{8,9},{9,8},{10,11... | collective-permute-start | bytes 393224 | tf_op jit(solution)/shard_map/ppermute | solution.py:108
  9.5 3.2 %copy-start.1 = (bf16[128,512]{1,0:T(8,128)(2,1)}, bf16[128,512]{1,0:T(8,128)(2,1)S(1)}, u32[]{:S(2)}) copy-start(bf16[128,512]{1,0:T(8,128)(2,1)S(1)} %collective-permute-done.1.refs_2_) | copy-start | bytes 393220
  9.5 3.1 %collective-permute-start.2 = (bf16[128,512]{1,0:T(8,128)(2,1)S(1)}, bf16[128,512]{1,0:T(8,128)(2,1)S(1)}, u32[]{:S(2)}, u32[]{:S(2)}) collective-permute-start(bf16[128,512]{1,0:T(8,128)(2,1)S(1)} %collective-permute-done.1.refs_2_), channel_id=1, source_target_pairs={{0,1},{1,0},{2,3},{3,2},{4,5},{5,4},{6,7},{7,6},{8,9},{9,8},{10,11... | collective-permute-start | bytes 393224 | tf_op jit(solution)/shard_map/ppermute | solution.py:108
  10.7 2.1 %copy-start.2 = (bf16[128,512]{1,0:T(8,128)(2,1)}, bf16[128,512]{1,0:T(8,128)(2,1)S(1)}, u32[]{:S(2)}) copy-start(bf16[128,512]{1,0:T(8,128)(2,1)S(1)} %collective-permute-done.5.refs_6_) | copy-start | bytes 393220
  10.7 2.0 %collective-permute-start.6 = (bf16[128,512]{1,0:T(8,128)(2,1)S(1)}, bf16[128,512]{1,0:T(8,128)(2,1)S(1)}, u32[]{:S(2)}, u32[]{:S(2)}) collective-permute-start(bf16[128,512]{1,0:T(8,128)(2,1)S(1)} %collective-permute-done.5.refs_6_), channel_id=1, source_target_pairs={{0,1},{1,0},{2,3},{3,2},{4,5},{5,4},{6,7},{7,6},{8,9},{9,8},{10,11... | collective-permute-start | bytes 393224 | tf_op jit(solution)/shard_map/ppermute | solution.py:108
  12.7 0.6 copy-start.3
  12.7 0.7 copy-start.4
  12.7 0.7 copy-start.5
  13.4 0.6 copy-start.6
  84.9 4.2 %collective-permute-start.7 = (f32[4,4,7,32,128]{4,3,2,1,0:T(8,128)}, f32[4,4,7,32,128]{4,3,2,1,0:T(8,128)S(1)}, u32[]{:S(2)}, u32[]{:S(2)}) collective-permute-start(f32[4,4,7,32,128]{4,3,2,1,0:T(8,128)} %get-tuple-element.8), channel_id=1, source_target_pairs={{0,1},{1,0},{2,3},{3,2},{4,5},{5,4},{6,7},{7,6},{8,9},{9,8},{10,11... | collective-permute-start | bytes 5505032 | tf_op jit(solution)/shard_map/ppermute | solution.py:108
  91.0 13.0 %collective-permute-start.10 = (f32[2,2,7,32,128]{4,3,2,1,0:T(8,128)S(1)}, f32[2,2,7,32,128]{4,3,2,1,0:T(8,128)S(1)}, u32[]{:S(2)}, u32[]{:S(2)}) collective-permute-start(f32[2,2,7,32,128]{4,3,2,1,0:T(8,128)S(1)} %slice.65), channel_id=1, source_target_pairs={{0,4},{1,5},{2,6},{3,7},{4,0},{5,1},{6,2},{7,3},{8,12},{9,13},{10,... | collective-permute-start | bytes 1376264 | tf_op jit(solution)/shard_map/ppermute | solution.py:108
  93.0 12.8 %collective-permute-start.8 = (f32[2,2,7,32,128]{4,3,2,1,0:T(8,128)S(1)}, f32[2,2,7,32,128]{4,3,2,1,0:T(8,128)S(1)}, u32[]{:S(2)}, u32[]{:S(2)}) collective-permute-start(f32[2,2,7,32,128]{4,3,2,1,0:T(8,128)S(1)} %slice_bitcast_fusion), channel_id=1, source_target_pairs={{0,2},{1,3},{2,0},{3,1},{4,6},{5,7},{6,4},{7,5},{8,10},{9,11},{10,... | collective-permute-start | bytes 1376264 | tf_op jit(solution)/shard_map/ppermute | solution.py:108
  104.1 7.3 %collective-permute-start.11 = (f32[2,7,32,128]{3,2,1,0:T(8,128)S(1)}, f32[2,7,32,128]{3,2,1,0:T(8,128)S(1)}, u32[]{:S(2)}, u32[]{:S(2)}) collective-permute-start(f32[2,7,32,128]{3,2,1,0:T(8,128)S(1)} %slice_bitcast_fusion.2), channel_id=1, source_target_pairs={{0,2},{1,3},{2,0},{3,1},{4,6},{5,7},{6,4},{7,5},{8,10},{9,11},{10,... | collective-permute-start | bytes 688136 | tf_op jit(solution)/shard_map/ppermute | solution.py:108
  106.0 6.8 %collective-permute-start.9 = (f32[2,7,32,128]{3,2,1,0:T(8,128)S(1)}, f32[2,7,32,128]{3,2,1,0:T(8,128)S(1)}, u32[]{:S(2)}, u32[]{:S(2)}) collective-permute-start(f32[2,7,32,128]{3,2,1,0:T(8,128)S(1)} %slice_bitcast_fusion.4), channel_id=1, source_target_pairs={{0,4},{1,5},{2,6},{3,7},{4,0},{5,1},{6,2},{7,3},{8,12},{9,13},{10,... | collective-permute-start | bytes 688136 | tf_op jit(solution)/shard_map/ppermute | solution.py:108
  112.9 6.1 %collective-permute-start.12 = (f32[2,7,32,128]{3,2,1,0:T(8,128)S(1)}, f32[2,7,32,128]{3,2,1,0:T(8,128)S(1)}, u32[]{:S(2)}, u32[]{:S(2)}) collective-permute-start(f32[2,7,32,128]{3,2,1,0:T(8,128)S(1)} %slice.56), channel_id=1, source_target_pairs={{0,8},{8,0},{16,24},{24,16},{1,9},{9,1},{17,25},{25,17},{2,10},{10... | collective-permute-start | bytes 688136 | tf_op jit(solution)/shard_map/ppermute | solution.py:108
  119.1 7.0 %collective-permute-start.13 = (f32[1,7,32,128]{3,2,1,0:T(8,128)S(1)}, f32[1,7,32,128]{3,2,1,0:T(8,128)S(1)}, u32[]{:S(2)}, u32[]{:S(2)}) collective-permute-start(f32[1,7,32,128]{3,2,1,0:T(8,128)S(1)} %slice.69), channel_id=1, source_target_pairs={{0,16},{8,24},{16,0},{24,8},{1,17},{9,25},{17,1},{25,9},{2,18},{10... | collective-permute-start | bytes 344072 | tf_op jit(solution)/shard_map/ppermute | solution.py:108

commit v2 on v1

--- a/solution.py
+++ b/solution.py
@@ -7,65 +7,83 @@
 from jax.experimental.pallas import tpu as pltpu
 from jax.sharding import PartitionSpec as P
 
-ROWS_BY_ROWS = (((1,), (1,)), ((), ()))
-
-
-def contract_rows(left, right):
-    return lax.dot_general(left, right, ROWS_BY_ROWS, preferred_element_type=jnp.float32)
-
 
 def band_kernel(sizes, place_ref, lists_ref, *refs):
     aux_blocks, span, depth, edge, width, slots, groups = sizes
     coeff_refs, refs = refs[:slots], refs[slots:]
     integrals_ref, keep_ref, send_ref = refs[:3]
-    coeffs, chosen, integrals, half, total, band, load_sem, coeff_sem, out_sem = refs[3:]
+    coeffs, chosen, integrals, half, flipped, total, band, load_sem, coeff_sem, out_sem = refs[3:]
     orb, aux = place_ref[0], place_ref[1]
     rows = edge // groups
 
     def load(block, m):
-        return pltpu.make_async_copy(integrals_ref.at[block, m], integrals.at[m], load_sem.at[m])
+        into = integrals.at[block % 2, m]
+        return pltpu.make_async_copy(integrals_ref.at[block, m], into, load_sem.at[block % 2, m])
 
+    for m in range(span):
+        load(0, m).start()
     coeff_loads = [pltpu.make_async_copy(coeff_refs[s], coeffs.at[s], coeff_sem.at[s]) for s in range(slots)]
     for copy in coeff_loads:
         copy.start()
-    for m in range(span):
-        load(0, m).start()
     band[...] = jnp.zeros_like(band)
     for copy in coeff_loads:
         copy.wait()
 
     def step(block, carry):
+        @pl.when(block + 1 < aux_blocks)
+        def _():
+            for m in range(span):
+                load(block + 1, m).start()
+
         listed = [lists_ref[block, j] for j in range(span)]
         for n in range(span):
             chosen[n * edge : (n + 1) * edge, :] = coeffs[listed[n] ^ orb]
         for m in range(span):
             load(block, m).wait()
-            left = jnp.concatenate([integrals[m, n].reshape(depth * edge, edge) for n in range(span)], axis=1)
+        for m in range(span):
+            pieces = [integrals[block % 2, m, n].reshape(depth * edge, edge) for n in range(span)]
+            left = jnp.concatenate(pieces, axis=1)
             made = jnp.dot(left, chosen[...], preferred_element_type=jnp.float32).astype(jnp.bfloat16)
             for a in range(depth):
-                half[m * edge : (m + 1) * edge, a * width : (a + 1) * width] = made[a * edge : (a + 1) * edge]
+                piece = made[a * edge : (a + 1) * edge]
+                half[m * edge : (m + 1) * edge, a * width : (a + 1) * width] = piece
+                flipped[a * width : (a + 1) * width, m * edge : (m + 1) * edge] = piece.T
 
-            @pl.when(block + 1 < aux_blocks)
-            def _():
-                load(block + 1, m).start()
-
-        last = (span - 1) * edge
-        total[:, :last] = contract_rows(half[...], half[:last])
-        total[last:, last:] = contract_rows(half[last:], half[last:])
-        for m in range(span):
-            for n in range(m + 1):
-                piece = total[m * edge : (m + 1) * edge, n * edge : (n + 1) * edge]
-                pairs = [(m, n, piece)] if m == n else [(m, n, piece), (n, m, piece.T)]
-                for j, k, value in pairs:
-                    slot = listed[j] ^ orb
-                    offset = listed[k] - listed[j] + span
-                    for g in range(groups):
-                        place = (slot & 1, slot >> 1, g ^ aux, offset)
-                        band[place] += value[g * rows : (g + 1) * rows]
+        for i in range(span):
+            columns = [flipped[:, j * edge : (j + 1) * edge] for j in (i, (i + 1) % span)]
+            made = jnp.dot(
+                half[i * edge : (i + 1) * edge],
+                jnp.concatenate(columns, axis=1),
+                preferred_element_type=jnp.float32,
+            )
+            here = slice(i * edge, (i + 1) * edge)
+            total[here, here] = made[:, :edge]
+            if i + 1 < span:
+                total[here, (i + 1) * edge : (i + 2) * edge] = made[:, edge:]
+            else:
+                total[:edge, here] = made[:, edge:].T
+        for j in range(span):
+            for k in range(j, span):
+                place = (listed[j] ^ orb, listed[k] - listed[j] + span)
+                band[place] += total[j * edge : (j + 1) * edge, k * edge : (k + 1) * edge]
         return carry
 
     lax.fori_loop(0, aux_blocks, step, 0)
-    outs = [pltpu.make_async_copy(band.at[i], ref, out_sem.at[i]) for i, ref in enumerate((keep_ref, send_ref))]
+
+    for slot in range(slots):
+        for offset in range(1, span + 1):
+            row = slot ^ orb
+
+            @pl.when(row + offset < slots)
+            def _():
+                band[(row + offset) ^ orb, span - offset] = band[slot, span + offset].T
+
+    outs = []
+    for side, ref in enumerate((keep_ref, send_ref)):
+        for s in range(slots // 2):
+            for g in range(groups):
+                source = band.at[2 * s + side, :, pl.ds(g * rows, rows)]
+                outs.append(pltpu.make_async_copy(source, ref.at[s, g ^ aux], out_sem.at[side, s, g]))
     for copy in outs:
         copy.start()
     for copy in outs:
@@ -89,13 +107,14 @@
         scratch_shapes=[
             pltpu.VMEM((slots, edge, width), jnp.bfloat16),
             pltpu.VMEM((span * edge, width), jnp.bfloat16),
-            pltpu.VMEM((span, span, depth, edge, edge), jnp.bfloat16),
+            pltpu.VMEM((2, span, span, depth, edge, edge), jnp.bfloat16),
             pltpu.VMEM((span * edge, depth * width), jnp.bfloat16),
+            pltpu.VMEM((depth * width, span * edge), jnp.bfloat16),
             pltpu.VMEM((span * edge, span * edge), jnp.float32),
-            pltpu.VMEM((2,) + part, jnp.float32),
-            pltpu.SemaphoreType.DMA((span,)),
+            pltpu.VMEM((slots, offsets, edge, edge), jnp.float32),
+            pltpu.SemaphoreType.DMA((2, span)),
             pltpu.SemaphoreType.DMA((slots,)),
-            pltpu.SemaphoreType.DMA((2,)),
+            pltpu.SemaphoreType.DMA((2, slots // 2, groups)),
         ],
         compiler_params=pltpu.CompilerParams(vmem_limit_bytes=56 * 2**20),
         name="band_partials",

time: 127 us -> 105 us (0.83)
  Pallas kernels: 70.8 us -> 48.9 us
    pallas_call x1, Pallas kernels: 70.8 us -> 48.9 us  [band_partials(): pl.pallas_call(functools.partial(band_kernel, sizes), out_shape=[jax.Shap...]
where the time goes in v2:
time: 105 us
  Pallas kernels  48.9 us (47%)
  waiting for transfers between devices  33.1 us (32%)
  starting transfers between devices  16.2 us (15%)
  other arithmetic  3.45 us (3%)
  local copies, waits for them, and re-layouts  2.89 us (3%)
    pallas_call x1, Pallas kernels, band_partials(): pl.pallas_call(functools.partial(band_kernel, sizes), out_shape=[jax.Shap...  48.9 us
    ppermute x14, waiting for transfers between devices, swap(): return lax.ppermute(value, axis, [(i, i ^ bits) for i in range(size)])  33.1 us
    ppermute x14, starting transfers between devices, swap(): return lax.ppermute(value, axis, [(i, i ^ bits) for i in range(size)])  16.2 us
    unnamed x15, local copies, waits for them, and re-layouts  2.7 us
  transfers between devices with their start and end apart: 14, of which 9 were waited for; matrix products, arithmetic and copies ran while one was open for 2% of the time, Pallas kernels for 0%

profile of v2, /device:TPU:0, one launch (start us, length us, event | category | flops | bytes accessed | tf_op | source)
XLA Modules:
  0.0 104.7 jit_solution(18217960782641942758)
XLA Ops:
  0.0 3.0 %collective-permute-start.3 = (bf16[128,512]{1,0:T(8,128)(2,1)}, bf16[128,512]{1,0:T(8,128)(2,1)S(1)}, u32[]{:S(2)}, u32[]{:S(2)}) collective-permute-start(bf16[128,512]{1,0:T(8,128)(2,1)} %refs_0_.1), channel_id=1, source_target_pairs={{0,4},{1,5},{2,6},{3,7},{4,0},{5,1},{6,2},{7,3},{8,12},{9,13},{10,... | collective-permute-start | bytes 393224 | tf_op jit(solution)/shard_map/ppermute | solution.py:127
  3.0 1.5 %collective-permute-start.1 = (bf16[128,512]{1,0:T(8,128)(2,1)}, bf16[128,512]{1,0:T(8,128)(2,1)S(1)}, u32[]{:S(2)}, u32[]{:S(2)}) collective-permute-start(bf16[128,512]{1,0:T(8,128)(2,1)} %refs_0_.1), channel_id=1, source_target_pairs={{0,2},{1,3},{2,0},{3,1},{4,6},{5,7},{6,4},{7,5},{8,10},{9,11},{10,... | collective-permute-start | bytes 393224 | tf_op jit(solution)/shard_map/ppermute | solution.py:127
  4.5 2.2 %collective-permute-done.3.refs_4_ = bf16[128,512]{1,0:T(8,128)(2,1)S(1)} collective-permute-done((bf16[128,512]{1,0:T(8,128)(2,1)}, bf16[128,512]{1,0:T(8,128)(2,1)S(1)}, u32[]{:S(2)}, u32[]{:S(2)}) %collective-permute-start.3) | collective-permute-done | bytes 131104 | tf_op jit(solution)/shard_map/ppermute | solution.py:127
  6.7 2.9 %collective-permute-done.1.refs_2_ = bf16[128,512]{1,0:T(8,128)(2,1)S(1)} collective-permute-done((bf16[128,512]{1,0:T(8,128)(2,1)}, bf16[128,512]{1,0:T(8,128)(2,1)S(1)}, u32[]{:S(2)}, u32[]{:S(2)}) %collective-permute-start.1) | collective-permute-done | bytes 131104 | tf_op jit(solution)/shard_map/ppermute | solution.py:127
  9.5 1.1 %collective-permute-done.5.refs_6_ = bf16[128,512]{1,0:T(8,128)(2,1)S(1)} collective-permute-done((bf16[128,512]{1,0:T(8,128)(2,1)}, bf16[128,512]{1,0:T(8,128)(2,1)S(1)}, u32[]{:S(2)}, u32[]{:S(2)}) %collective-permute-start.5) | collective-permute-done | bytes 131104 | tf_op jit(solution)/shard_map/ppermute | solution.py:127
  10.7 1.4 %copy.5.lists_ref = s32[8,3]{1,0:T(8,128)} copy(s32[8,3]{0,1:T(4,128)} %param.4) | data formatting | bytes 192 | tf_op args[1]
  12.0 0.6 pad_add_fusion.place_ref
  12.7 0.6 copy-done.3
  13.4 0.6 copy-done.6
  14.1 48.9 %band_partials.1 = (f32[4,4,7,32,128]{4,3,2,1,0:T(8,128)}, f32[4,4,7,32,128]{4,3,2,1,0:T(8,128)}) custom-call(s32[2]{0:T(128)} %pad_add_fusion.place_ref, s32[8,3]{1,0:T(8,128)} %copy.5.lists_ref, bf16[128,512]{1,0:T(8,128)(2,1)} %refs_0_.1, bf16[128,512]{1,0:T(8,128)(2,1)} %copy-done.3, bf16[128,512]{1,0:T(8,128)(2,1)} %copy-done.1, ...), custom_call_target="tpu_custom_call" | custom-call | tf_op jit(solution)/shard_map/band_partials/pallas_call | solution.py:102
  63.5 3.6 %collective-permute-done.7 = f32[4,4,7,32,128]{4,3,2,1,0:T(8,128)S(1)} collective-permute-done((f32[4,4,7,32,128]{4,3,2,1,0:T(8,128)}, f32[4,4,7,32,128]{4,3,2,1,0:T(8,128)S(1)}, u32[]{:S(2)}, u32[]{:S(2)}) %collective-permute-start.7) | collective-permute-done | bytes 1835040 | tf_op jit(solution)/shard_map/ppermute | solution.py:127
  67.1 1.9 %add.21 = f32[4,4,7,32,128]{4,3,2,1,0:T(8,128)S(1)} add(f32[4,4,7,32,128]{4,3,2,1,0:T(8,128)} %get-tuple-element.7, f32[4,4,7,32,128]{4,3,2,1,0:T(8,128)S(1)} %collective-permute-done.7) | non-fusion elementwise | flops 458752 | bytes 5505024 | tf_op jit(solution)/shard_map/add | solution.py:137
  69.1 1.8 %collective-permute-start.10 = (f32[2,2,7,32,128]{4,3,2,1,0:T(8,128)S(1)}, f32[2,2,7,32,128]{4,3,2,1,0:T(8,128)S(1)}, u32[]{:S(2)}, u32[]{:S(2)}) collective-permute-start(f32[2,2,7,32,128]{4,3,2,1,0:T(8,128)S(1)} %slice.65), channel_id=1, source_target_pairs={{0,4},{1,5},{2,6},{3,7},{4,0},{5,1},{6,2},{7,3},{8,12},{9,13},{10,... | collective-permute-start | bytes 1376264 | tf_op jit(solution)/shard_map/ppermute | solution.py:127
  71.0 1.6 %collective-permute-start.8 = (f32[2,2,7,32,128]{4,3,2,1,0:T(8,128)S(1)}, f32[2,2,7,32,128]{4,3,2,1,0:T(8,128)S(1)}, u32[]{:S(2)}, u32[]{:S(2)}) collective-permute-start(f32[2,2,7,32,128]{4,3,2,1,0:T(8,128)S(1)} %slice_bitcast_fusion), channel_id=1, source_target_pairs={{0,2},{1,3},{2,0},{3,1},{4,6},{5,7},{6,4},{7,5},{8,10},{9,11},{10,... | collective-permute-start | bytes 1376264 | tf_op jit(solution)/shard_map/ppermute | solution.py:127
  72.6 9.4 %collective-permute-done.10 = f32[2,2,7,32,128]{4,3,2,1,0:T(8,128)S(1)} collective-permute-done((f32[2,2,7,32,128]{4,3,2,1,0:T(8,128)S(1)}, f32[2,2,7,32,128]{4,3,2,1,0:T(8,128)S(1)}, u32[]{:S(2)}, u32[]{:S(2)}) %collective-permute-start.10) | collective-permute-done | bytes 458784 | tf_op jit(solution)/shard_map/ppermute | solution.py:127
  82.0 1.8 %collective-permute-start.11 = (f32[2,7,32,128]{3,2,1,0:T(8,128)S(1)}, f32[2,7,32,128]{3,2,1,0:T(8,128)S(1)}, u32[]{:S(2)}, u32[]{:S(2)}) collective-permute-start(f32[2,7,32,128]{3,2,1,0:T(8,128)S(1)} %slice_bitcast_fusion.2), channel_id=1, source_target_pairs={{0,2},{1,3},{2,0},{3,1},{4,6},{5,7},{6,4},{7,5},{8,10},{9,11},{10,... | collective-permute-start | bytes 688136 | tf_op jit(solution)/shard_map/ppermute | solution.py:127
  83.9 1.6 %collective-permute-start.9 = (f32[2,7,32,128]{3,2,1,0:T(8,128)S(1)}, f32[2,7,32,128]{3,2,1,0:T(8,128)S(1)}, u32[]{:S(2)}, u32[]{:S(2)}) collective-permute-start(f32[2,7,32,128]{3,2,1,0:T(8,128)S(1)} %slice_bitcast_fusion.4), channel_id=1, source_target_pairs={{0,4},{1,5},{2,6},{3,7},{4,0},{5,1},{6,2},{7,3},{8,12},{9,13},{10,... | collective-permute-start | bytes 688136 | tf_op jit(solution)/shard_map/ppermute | solution.py:127
  85.5 3.7 %collective-permute-done.11 = f32[2,7,32,128]{3,2,1,0:T(8,128)S(1)} collective-permute-done((f32[2,7,32,128]{3,2,1,0:T(8,128)S(1)}, f32[2,7,32,128]{3,2,1,0:T(8,128)S(1)}, u32[]{:S(2)}, u32[]{:S(2)}) %collective-permute-start.11) | collective-permute-done | bytes 229408 | tf_op jit(solution)/shard_map/ppermute | solution.py:127
  89.2 1.6 %collective-permute-done.9 = f32[2,7,32,128]{3,2,1,0:T(8,128)S(1)} collective-permute-done((f32[2,7,32,128]{3,2,1,0:T(8,128)S(1)}, f32[2,7,32,128]{3,2,1,0:T(8,128)S(1)}, u32[]{:S(2)}, u32[]{:S(2)}) %collective-permute-start.9) | collective-permute-done | bytes 229408 | tf_op jit(solution)/shard_map/ppermute | solution.py:127
  90.9 1.6 %collective-permute-start.12 = (f32[2,7,32,128]{3,2,1,0:T(8,128)S(1)}, f32[2,7,32,128]{3,2,1,0:T(8,128)S(1)}, u32[]{:S(2)}, u32[]{:S(2)}) collective-permute-start(f32[2,7,32,128]{3,2,1,0:T(8,128)S(1)} %slice.56), channel_id=1, source_target_pairs={{0,8},{8,0},{16,24},{24,16},{1,9},{9,1},{17,25},{25,17},{2,10},{10... | collective-permute-start | bytes 688136 | tf_op jit(solution)/shard_map/ppermute | solution.py:127
  92.5 4.4 %collective-permute-done.12 = f32[2,7,32,128]{3,2,1,0:T(8,128)S(1)} collective-permute-done((f32[2,7,32,128]{3,2,1,0:T(8,128)S(1)}, f32[2,7,32,128]{3,2,1,0:T(8,128)S(1)}, u32[]{:S(2)}, u32[]{:S(2)}) %collective-permute-start.12) | collective-permute-done | bytes 229408 | tf_op jit(solution)/shard_map/ppermute | solution.py:127
  97.0 2.8 %collective-permute-start.13 = (f32[1,7,32,128]{3,2,1,0:T(8,128)S(1)}, f32[1,7,32,128]{3,2,1,0:T(8,128)S(1)}, u32[]{:S(2)}, u32[]{:S(2)}) collective-permute-start(f32[1,7,32,128]{3,2,1,0:T(8,128)S(1)} %slice.69), channel_id=1, source_target_pairs={{0,16},{8,24},{16,0},{24,8},{1,17},{9,25},{17,1},{25,9},{2,18},{10... | collective-permute-start | bytes 344072 | tf_op jit(solution)/shard_map/ppermute | solution.py:127
  99.8 4.2 %collective-permute-done.13 = f32[1,7,32,128]{3,2,1,0:T(8,128)S(1)} collective-permute-done((f32[1,7,32,128]{3,2,1,0:T(8,128)S(1)}, f32[1,7,32,128]{3,2,1,0:T(8,128)S(1)}, u32[]{:S(2)}, u32[]{:S(2)}) %collective-permute-start.13) | collective-permute-done | bytes 114720 | tf_op jit(solution)/shard_map/ppermute | solution.py:127
  104.0 0.7 copy_bitcast_fusion
  (36 shorter events, 1.1 us)
Async XLA Ops:
  0.0 6.7 %collective-permute-start.3 = (bf16[128,512]{1,0:T(8,128)(2,1)}, bf16[128,512]{1,0:T(8,128)(2,1)S(1)}, u32[]{:S(2)}, u32[]{:S(2)}) collective-permute-start(bf16[128,512]{1,0:T(8,128)(2,1)} %refs_0_.1), channel_id=1, source_target_pairs={{0,4},{1,5},{2,6},{3,7},{4,0},{5,1},{6,2},{7,3},{8,12},{9,13},{10,... | collective-permute-start | bytes 393224 | tf_op jit(solution)/shard_map/ppermute | solution.py:127
  3.0 6.6 %collective-permute-start.1 = (bf16[128,512]{1,0:T(8,128)(2,1)}, bf16[128,512]{1,0:T(8,128)(2,1)S(1)}, u32[]{:S(2)}, u32[]{:S(2)}) collective-permute-start(bf16[128,512]{1,0:T(8,128)(2,1)} %refs_0_.1), channel_id=1, source_target_pairs={{0,2},{1,3},{2,0},{3,1},{4,6},{5,7},{6,4},{7,5},{8,10},{9,11},{10,... | collective-permute-start | bytes 393224 | tf_op jit(solution)/shard_map/ppermute | solution.py:127
  4.5 6.2 %collective-permute-start.5 = (bf16[128,512]{1,0:T(8,128)(2,1)}, bf16[128,512]{1,0:T(8,128)(2,1)S(1)}, u32[]{:S(2)}, u32[]{:S(2)}) collective-permute-start(bf16[128,512]{1,0:T(8,128)(2,1)} %refs_0_.1), channel_id=1, source_target_pairs={{0,6},{1,7},{2,4},{3,5},{4,2},{5,3},{6,0},{7,1},{8,14},{9,15},{10,... | collective-permute-start | bytes 393224 | tf_op jit(solution)/shard_map/ppermute | solution.py:127
  4.5 8.2 %collective-permute-start = (bf16[128,512]{1,0:T(8,128)(2,1)}, bf16[128,512]{1,0:T(8,128)(2,1)S(1)}, u32[]{:S(2)}, u32[]{:S(2)}) collective-permute-start(bf16[128,512]{1,0:T(8,128)(2,1)} %refs_0_.1), channel_id=1, source_target_pairs={{0,1},{1,0},{2,3},{3,2},{4,5},{5,4},{6,7},{7,6},{8,9},{9,8},{10,11... | collective-permute-start | bytes 393224 | tf_op jit(solution)/shard_map/ppermute | solution.py:127
  6.7 6.0 %copy-start = (bf16[128,512]{1,0:T(8,128)(2,1)}, bf16[128,512]{1,0:T(8,128)(2,1)S(1)}, u32[]{:S(2)}) copy-start(bf16[128,512]{1,0:T(8,128)(2,1)S(1)} %collective-permute-done.3.refs_4_) | copy-start | bytes 393220
  6.7 6.0 %collective-permute-start.4 = (bf16[128,512]{1,0:T(8,128)(2,1)S(1)}, bf16[128,512]{1,0:T(8,128)(2,1)S(1)}, u32[]{:S(2)}, u32[]{:S(2)}) collective-permute-start(bf16[128,512]{1,0:T(8,128)(2,1)S(1)} %collective-permute-done.3.refs_4_), channel_id=1, source_target_pairs={{0,1},{1,0},{2,3},{3,2},{4,5},{5,4},{6,7},{7,6},{8,9},{9,8},{10,11... | collective-permute-start | bytes 393224 | tf_op jit(solution)/shard_map/ppermute | solution.py:127
  9.5 3.2 %copy-start.1 = (bf16[128,512]{1,0:T(8,128)(2,1)}, bf16[128,512]{1,0:T(8,128)(2,1)S(1)}, u32[]{:S(2)}) copy-start(bf16[128,512]{1,0:T(8,128)(2,1)S(1)} %collective-permute-done.1.refs_2_) | copy-start | bytes 393220
  9.5 3.1 %collective-permute-start.2 = (bf16[128,512]{1,0:T(8,128)(2,1)S(1)}, bf16[128,512]{1,0:T(8,128)(2,1)S(1)}, u32[]{:S(2)}, u32[]{:S(2)}) collective-permute-start(bf16[128,512]{1,0:T(8,128)(2,1)S(1)} %collective-permute-done.1.refs_2_), channel_id=1, source_target_pairs={{0,1},{1,0},{2,3},{3,2},{4,5},{5,4},{6,7},{7,6},{8,9},{9,8},{10,11... | collective-permute-start | bytes 393224 | tf_op jit(solution)/shard_map/ppermute | solution.py:127
  10.7 2.1 %copy-start.2 = (bf16[128,512]{1,0:T(8,128)(2,1)}, bf16[128,512]{1,0:T(8,128)(2,1)S(1)}, u32[]{:S(2)}) copy-start(bf16[128,512]{1,0:T(8,128)(2,1)S(1)} %collective-permute-done.5.refs_6_) | copy-start | bytes 393220
  10.7 2.0 %collective-permute-start.6 = (bf16[128,512]{1,0:T(8,128)(2,1)S(1)}, bf16[128,512]{1,0:T(8,128)(2,1)S(1)}, u32[]{:S(2)}, u32[]{:S(2)}) collective-permute-start(bf16[128,512]{1,0:T(8,128)(2,1)S(1)} %collective-permute-done.5.refs_6_), channel_id=1, source_target_pairs={{0,1},{1,0},{2,3},{3,2},{4,5},{5,4},{6,7},{7,6},{8,9},{9,8},{10,11... | collective-permute-start | bytes 393224 | tf_op jit(solution)/shard_map/ppermute | solution.py:127
  12.7 0.6 copy-start.3
  12.7 0.7 copy-start.4
  12.7 0.7 copy-start.5
  13.4 0.6 copy-start.6
  63.0 4.2 %collective-permute-start.7 = (f32[4,4,7,32,128]{4,3,2,1,0:T(8,128)}, f32[4,4,7,32,128]{4,3,2,1,0:T(8,128)S(1)}, u32[]{:S(2)}, u32[]{:S(2)}) collective-permute-start(f32[4,4,7,32,128]{4,3,2,1,0:T(8,128)} %get-tuple-element.8), channel_id=1, source_target_pairs={{0,1},{1,0},{2,3},{3,2},{4,5},{5,4},{6,7},{7,6},{8,9},{9,8},{10,11... | collective-permute-start | bytes 5505032 | tf_op jit(solution)/shard_map/ppermute | solution.py:127
  69.1 12.9 %collective-permute-start.10 = (f32[2,2,7,32,128]{4,3,2,1,0:T(8,128)S(1)}, f32[2,2,7,32,128]{4,3,2,1,0:T(8,128)S(1)}, u32[]{:S(2)}, u32[]{:S(2)}) collective-permute-start(f32[2,2,7,32,128]{4,3,2,1,0:T(8,128)S(1)} %slice.65), channel_id=1, source_target_pairs={{0,4},{1,5},{2,6},{3,7},{4,0},{5,1},{6,2},{7,3},{8,12},{9,13},{10,... | collective-permute-start | bytes 1376264 | tf_op jit(solution)/shard_map/ppermute | solution.py:127
  71.0 12.8 %collective-permute-start.8 = (f32[2,2,7,32,128]{4,3,2,1,0:T(8,128)S(1)}, f32[2,2,7,32,128]{4,3,2,1,0:T(8,128)S(1)}, u32[]{:S(2)}, u32[]{:S(2)}) collective-permute-start(f32[2,2,7,32,128]{4,3,2,1,0:T(8,128)S(1)} %slice_bitcast_fusion), channel_id=1, source_target_pairs={{0,2},{1,3},{2,0},{3,1},{4,6},{5,7},{6,4},{7,5},{8,10},{9,11},{10,... | collective-permute-start | bytes 1376264 | tf_op jit(solution)/shard_map/ppermute | solution.py:127
  82.0 7.1 %collective-permute-start.11 = (f32[2,7,32,128]{3,2,1,0:T(8,128)S(1)}, f32[2,7,32,128]{3,2,1,0:T(8,128)S(1)}, u32[]{:S(2)}, u32[]{:S(2)}) collective-permute-start(f32[2,7,32,128]{3,2,1,0:T(8,128)S(1)} %slice_bitcast_fusion.2), channel_id=1, source_target_pairs={{0,2},{1,3},{2,0},{3,1},{4,6},{5,7},{6,4},{7,5},{8,10},{9,11},{10,... | collective-permute-start | bytes 688136 | tf_op jit(solution)/shard_map/ppermute | solution.py:127
  83.9 6.8 %collective-permute-start.9 = (f32[2,7,32,128]{3,2,1,0:T(8,128)S(1)}, f32[2,7,32,128]{3,2,1,0:T(8,128)S(1)}, u32[]{:S(2)}, u32[]{:S(2)}) collective-permute-start(f32[2,7,32,128]{3,2,1,0:T(8,128)S(1)} %slice_bitcast_fusion.4), channel_id=1, source_target_pairs={{0,4},{1,5},{2,6},{3,7},{4,0},{5,1},{6,2},{7,3},{8,12},{9,13},{10,... | collective-permute-start | bytes 688136 | tf_op jit(solution)/shard_map/ppermute | solution.py:127
  90.9 6.1 %collective-permute-start.12 = (f32[2,7,32,128]{3,2,1,0:T(8,128)S(1)}, f32[2,7,32,128]{3,2,1,0:T(8,128)S(1)}, u32[]{:S(2)}, u32[]{:S(2)}) collective-permute-start(f32[2,7,32,128]{3,2,1,0:T(8,128)S(1)} %slice.56), channel_id=1, source_target_pairs={{0,8},{8,0},{16,24},{24,16},{1,9},{9,1},{17,25},{25,17},{2,10},{10... | collective-permute-start | bytes 688136 | tf_op jit(solution)/shard_map/ppermute | solution.py:127
  97.0 7.0 %collective-permute-start.13 = (f32[1,7,32,128]{3,2,1,0:T(8,128)S(1)}, f32[1,7,32,128]{3,2,1,0:T(8,128)S(1)}, u32[]{:S(2)}, u32[]{:S(2)}) collective-permute-start(f32[1,7,32,128]{3,2,1,0:T(8,128)S(1)} %slice.69), channel_id=1, source_target_pairs={{0,16},{8,24},{16,0},{24,8},{1,17},{9,25},{17,1},{25,9},{2,18},{10... | collective-permute-start | bytes 344072 | tf_op jit(solution)/shard_map/ppermute | solution.py:127

commit v3 on v2

--- a/solution.py
+++ b/solution.py
@@ -1,4 +1,5 @@
 import functools
+import math
 
 import jax
 import jax.numpy as jnp
@@ -8,12 +9,12 @@
 from jax.sharding import PartitionSpec as P
 
 
-def band_kernel(sizes, place_ref, lists_ref, *refs):
+def band_kernel(sizes, lists_ref, *refs):
     aux_blocks, span, depth, edge, width, slots, groups = sizes
     coeff_refs, refs = refs[:slots], refs[slots:]
     integrals_ref, keep_ref, send_ref = refs[:3]
     coeffs, chosen, integrals, half, flipped, total, band, load_sem, coeff_sem, out_sem = refs[3:]
-    orb, aux = place_ref[0], place_ref[1]
+    orb, aux = lax.axis_index("orb"), lax.axis_index("aux")
     rows = edge // groups
 
     def load(block, m):
@@ -90,7 +91,7 @@
         copy.wait()
 
 
-def band_partials(place, block_lists, coeff_slots, three_centre, groups):
+def band_partials(block_lists, coeff_slots, three_centre, groups):
     aux_blocks, span, _, depth, edge, _ = three_centre.shape
     width = coeff_slots[0].shape[1]
     slots = len(coeff_slots)
@@ -99,26 +100,58 @@
     part = (slots // 2, groups, offsets, edge // groups, edge)
     anywhere = pl.BlockSpec(memory_space=pl.ANY)
     scalars = pl.BlockSpec(memory_space=pltpu.SMEM)
+    buffers = [
+        pltpu.VMEM((slots, edge, width), jnp.bfloat16),
+        pltpu.VMEM((span * edge, width), jnp.bfloat16),
+        pltpu.VMEM((2, span, span, depth, edge, edge), jnp.bfloat16),
+        pltpu.VMEM((span * edge, depth * width), jnp.bfloat16),
+        pltpu.VMEM((depth * width, span * edge), jnp.bfloat16),
+        pltpu.VMEM((span * edge, span * edge), jnp.float32),
+        pltpu.VMEM((slots, offsets, edge, edge), jnp.float32),
+    ]
+    held = sum(math.prod(b.shape) * jnp.dtype(b.dtype).itemsize for b in buffers)
     return pl.pallas_call(
         functools.partial(band_kernel, sizes),
         out_shape=[jax.ShapeDtypeStruct(part, jnp.float32)] * 2,
-        in_specs=[scalars, scalars] + [anywhere] * (slots + 1),
+        in_specs=[scalars] + [anywhere] * (slots + 1),
         out_specs=[anywhere] * 2,
-        scratch_shapes=[
-            pltpu.VMEM((slots, edge, width), jnp.bfloat16),
-            pltpu.VMEM((span * edge, width), jnp.bfloat16),
-            pltpu.VMEM((2, span, span, depth, edge, edge), jnp.bfloat16),
-            pltpu.VMEM((span * edge, depth * width), jnp.bfloat16),
-            pltpu.VMEM((depth * width, span * edge), jnp.bfloat16),
-            pltpu.VMEM((span * edge, span * edge), jnp.float32),
-            pltpu.VMEM((slots, offsets, edge, edge), jnp.float32),
+        scratch_shapes=buffers
+        + [
             pltpu.SemaphoreType.DMA((2, span)),
             pltpu.SemaphoreType.DMA((slots,)),
             pltpu.SemaphoreType.DMA((2, slots // 2, groups)),
         ],
-        compiler_params=pltpu.CompilerParams(vmem_limit_bytes=56 * 2**20),
+        compiler_params=pltpu.CompilerParams(vmem_limit_bytes=held + 8 * 2**20),
         name="band_partials",
-    )(place, block_lists, *coeff_slots, three_centre)
+    )(block_lists, *coeff_slots, three_centre)
+
+
+LEVELS = 32767
+STEPS = 64
+LIFT = 30
+FLOOR = -100
+
+
+def encode(value):
+    lead, (offsets, rows, lanes) = value.shape[:-3], value.shape[-3:]
+    lifted = value * 2.0**LIFT
+    top = jnp.max(jnp.abs(lifted), axis=-2, keepdims=True)
+    exponent = jnp.log2(jnp.maximum(top, 2.0 ** (FLOOR + 15))) - 15.0
+    exponent = jnp.floor(exponent * STEPS) + 2.0
+    scaled = lifted * jnp.exp2(exponent * (-1.0 / STEPS))
+    coded = jnp.clip(jnp.round(scaled), -LEVELS, LEVELS).astype(jnp.int16)
+    coded = coded.reshape(lead + (offsets * rows, lanes))
+    scales = exponent.astype(jnp.int16).reshape(lead + (offsets, lanes))
+    blank = jnp.zeros(lead + (-offsets % 16, lanes), jnp.int16)
+    return jnp.concatenate([coded, scales, blank], axis=-2)
+
+
+def decode(coded, offsets, rows):
+    lead, lanes = coded.shape[:-2], coded.shape[-1]
+    values = coded[..., : offsets * rows, :].reshape(lead + (offsets, rows, lanes)).astype(jnp.float32)
+    exponent = coded[..., offsets * rows : offsets * (rows + 1), :].astype(jnp.float32)
+    scale = jnp.exp2(exponent * (1.0 / STEPS)) * 2.0**-LIFT
+    return values * scale.reshape(lead + (offsets, 1, lanes))
 
 
 def per_device(orb_size, aux_size, three_centre, block_lists, occupied):
@@ -126,13 +159,17 @@
         size = {"orb": orb_size, "aux": aux_size}[axis]
         return lax.ppermute(value, axis, [(i, i ^ bits) for i in range(size)])
 
-    place = jnp.stack([lax.axis_index("orb"), lax.axis_index("aux")]).astype(jnp.int32)
+    def swap_sums(value, axis, bits):
+        return decode(swap(encode(value), axis, bits), *value.shape[-3:-1])
+
     slots = {0: occupied, 1: swap(occupied, "orb", 1)}
     for s in range(2, orb_size, 2):
         slots[s] = swap(occupied, "orb", s)
+    arrived, block_lists = lax.optimization_barrier(([slots[s] for s in range(2, orb_size, 2)], block_lists + 0))
     for s in range(2, orb_size, 2):
+        slots[s] = arrived[s // 2 - 1]
         slots[s + 1] = swap(slots[s], "orb", 1)
-    keep, send = band_partials(place, block_lists, [slots[s] for s in range(orb_size)], three_centre, aux_size)
+    keep, send = band_partials(block_lists, [slots[s] for s in range(orb_size)], three_centre, aux_size)
 
     summed = keep + swap(send, "orb", 1)
     bits = list(range(1, orb_size.bit_length() - 1))
@@ -144,13 +181,13 @@
         for bit in bits if part == 0 else left[:]:
             axis = left.index(bit)
             kept = lax.index_in_dim(taken, 0, axis, keepdims=False)
-            taken = kept + swap(lax.index_in_dim(taken, 1, axis, keepdims=False), "orb", 1 << bit)
+            taken = kept + swap_sums(lax.index_in_dim(taken, 1, axis, keepdims=False), "orb", 1 << bit)
             left.remove(bit)
         halves.append(taken)
     rows = jnp.concatenate(halves, axis=0)
     step = 1
     while step < aux_size:
-        rows = rows[0::2] + swap(rows[1::2], "aux", step)
+        rows = rows[0::2] + swap_sums(rows[1::2], "aux", step)
         step *= 2
     return jnp.transpose(rows, (0, 2, 1, 3)).reshape(1, rows.shape[2], rows.shape[1] * rows.shape[3])
 

time: 105 us -> 93.1 us (0.89)
  waiting for transfers between devices: 33.1 us -> 26.1 us
  Pallas kernels: 48.9 us -> 47.3 us
  starting transfers between devices: 16.2 us -> 14.7 us
    ppermute x14, waiting for transfers between devices: 33.1 us -> 26.1 us  [swap(): return lax.ppermute(value, axis, [(i, i ^ bits) for i in range(size)])]
    unnamed x15 -> x2, local copies, waits for them, and re-layouts: 2.7 us -> 0.9 us
    pallas_call x1, Pallas kernels: 48.9 us -> 47.3 us  [band_partials(): pl.pallas_call(functools.partial(band_kernel, sizes), out_shape=[jax.Shap...]
    ppermute x14, starting transfers between devices: 16.2 us -> 14.7 us  [swap(): return lax.ppermute(value, axis, [(i, i ^ bits) for i in range(size)])]
    add x1, other arithmetic: 1.91 us -> 0.41 us  [per_device(): summed = keep + swap(send, 'orb', 1)]
  transfers between devices with their start and end apart: 14 -> 14, of which waited for: 9 -> 12; matrix products, arithmetic and copies ran while one was open for 2% -> 1% of each run, Pallas kernels for 0% -> 0%
where the time goes in v3:
time: 93.1 us; the launch traced here: 92.9 us
  Pallas kernels  47.3 us (51%)
  waiting for transfers between devices  26.1 us (28%)
  starting transfers between devices  14.7 us (16%)
  other arithmetic  2.72 us (3%)
  local copies, waits for them, and re-layouts  1.86 us (2%)
    pallas_call x1, Pallas kernels, band_partials(): pl.pallas_call(functools.partial(band_kernel, sizes), out_shape=[jax.Shap...  47.3 us
    ppermute x14, waiting for transfers between devices, swap(): return lax.ppermute(value, axis, [(i, i ^ bits) for i in range(size)])  26.1 us
    ppermute x14, starting transfers between devices, swap(): return lax.ppermute(value, axis, [(i, i ^ bits) for i in range(size)])  14.7 us
  transfers between devices with their start and end apart: 14, of which 12 were waited for; matrix products, arithmetic and copies ran while one was open for 1% of the time, Pallas kernels for 0%

profile of v3, /device:TPU:0, one launch (start us, length us, event | category | flops | bytes accessed | tf_op | source)
XLA Modules:
  0.0 92.9 jit_solution(2497629759006856375)
XLA Ops:
  0.0 2.9 %collective-permute-start = (bf16[128,512]{1,0:T(8,128)(2,1)}, bf16[128,512]{1,0:T(8,128)(2,1)S(1)}, u32[]{:S(2)}, u32[]{:S(2)}) collective-permute-start(bf16[128,512]{1,0:T(8,128)(2,1)} %refs_0_.1), channel_id=1, source_target_pairs={{0,2},{1,3},{2,0},{3,1},{4,6},{5,7},{6,4},{7,5},{8,10},{9,11},{10,... | collective-permute-start | bytes 393224 | tf_op jit(solution)/shard_map/ppermute | solution.py:160
  2.9 1.5 %collective-permute-start.1 = (bf16[128,512]{1,0:T(8,128)(2,1)}, bf16[128,512]{1,0:T(8,128)(2,1)S(1)}, u32[]{:S(2)}, u32[]{:S(2)}) collective-permute-start(bf16[128,512]{1,0:T(8,128)(2,1)} %refs_0_.1), channel_id=1, source_target_pairs={{0,4},{1,5},{2,6},{3,7},{4,0},{5,1},{6,2},{7,3},{8,12},{9,13},{10,... | collective-permute-start | bytes 393224 | tf_op jit(solution)/shard_map/ppermute | solution.py:160
  4.5 2.7 %collective-permute-done.refs_2_ = bf16[128,512]{1,0:T(8,128)(2,1)S(1)} collective-permute-done((bf16[128,512]{1,0:T(8,128)(2,1)}, bf16[128,512]{1,0:T(8,128)(2,1)S(1)}, u32[]{:S(2)}, u32[]{:S(2)}) %collective-permute-start) | collective-permute-done | bytes 131104 | tf_op jit(solution)/shard_map/ppermute | solution.py:160
  7.2 3.8 %collective-permute-done.1.refs_4_ = bf16[128,512]{1,0:T(8,128)(2,1)S(1)} collective-permute-done((bf16[128,512]{1,0:T(8,128)(2,1)}, bf16[128,512]{1,0:T(8,128)(2,1)S(1)}, u32[]{:S(2)}, u32[]{:S(2)}) %collective-permute-start.1) | collective-permute-done | bytes 131104 | tf_op jit(solution)/shard_map/ppermute | solution.py:160
  10.9 0.5 collective-permute-start.5
  11.4 0.8 copy.5.lists_ref
  12.5 0.3 collective-permute-done.6.refs_7_
  12.8 0.9 copy-done
  13.7 47.3 %band_partials.1 = (f32[4,4,7,32,128]{4,3,2,1,0:T(8,128)S(1)}, f32[4,4,7,32,128]{4,3,2,1,0:T(8,128)S(1)}) custom-call(s32[8,3]{1,0:T(8,128)S(1)} %copy.5.lists_ref, bf16[128,512]{1,0:T(8,128)(2,1)S(1)} %copy-done, bf16[128,512]{1,0:T(8,128)(2,1)S(1)} %collective-permute-done.3.refs_1_, bf16[128,512]{1,0:T(8,128)(2,1)S(1)} %collective-permute-done.refs_2_, ...), custom_call_target="tpu_custom_call" | custom-call | tf_op jit(solution)/shard_map/band_partials/pallas_call | solution.py:113
  61.4 3.5 %collective-permute-done.7 = f32[4,4,7,32,128]{4,3,2,1,0:T(8,128)S(1)} collective-permute-done((f32[4,4,7,32,128]{4,3,2,1,0:T(8,128)S(1)}, f32[4,4,7,32,128]{4,3,2,1,0:T(8,128)S(1)}, u32[]{:S(2)}, u32[]{:S(2)}) %collective-permute-start.7) | collective-permute-done | bytes 1835040 | tf_op jit(solution)/shard_map/ppermute | solution.py:160
  64.9 0.4 add.149
  65.9 1.3 %collective-permute-start.8 = (s16[2,2,240,128]{3,2,1,0:T(8,128)(2,1)S(1)}, s16[2,2,240,128]{3,2,1,0:T(8,128)(2,1)S(1)}, u32[]{:S(2)}, u32[]{:S(2)}) collective-permute-start(s16[2,2,240,128]{3,2,1,0:T(8,128)(2,1)S(1)} %get-tuple-element.37), channel_id=1, source_target_pairs={{0,2},{1,3},{2,0},{3,1},{4,6},{5,7},{6,4},{7,5},{8,10},{9,11},{10,... | collective-permute-start | bytes 737288 | tf_op jit(solution)/shard_map/ppermute | solution.py:160
  67.2 0.8 collective-permute-start.10
  68.0 6.0 %collective-permute-done.8 = s16[2,2,240,128]{3,2,1,0:T(8,128)(2,1)S(1)} collective-permute-done((s16[2,2,240,128]{3,2,1,0:T(8,128)(2,1)S(1)}, s16[2,2,240,128]{3,2,1,0:T(8,128)(2,1)S(1)}, u32[]{:S(2)}, u32[]{:S(2)}) %collective-permute-start.8) | collective-permute-done | bytes 245792 | tf_op jit(solution)/shard_map/ppermute | solution.py:160
  74.2 0.7 collective-permute-done.10
  75.4 0.9 collective-permute-start.11
  76.3 1.5 %collective-permute-start.9 = (s16[2,240,128]{2,1,0:T(8,128)(2,1)S(1)}, s16[2,240,128]{2,1,0:T(8,128)(2,1)S(1)}, u32[]{:S(2)}, u32[]{:S(2)}) collective-permute-start(s16[2,240,128]{2,1,0:T(8,128)(2,1)S(1)} %get-tuple-element.35), channel_id=1, source_target_pairs={{0,4},{1,5},{2,6},{3,7},{4,0},{5,1},{6,2},{7,3},{8,12},{9,13},{10,... | collective-permute-start | bytes 368648 | tf_op jit(solution)/shard_map/ppermute | solution.py:160
  77.8 2.6 %collective-permute-done.11 = s16[2,240,128]{2,1,0:T(8,128)(2,1)S(1)} collective-permute-done((s16[2,240,128]{2,1,0:T(8,128)(2,1)S(1)}, s16[2,240,128]{2,1,0:T(8,128)(2,1)S(1)}, u32[]{:S(2)}, u32[]{:S(2)}) %collective-permute-start.11) | collective-permute-done | bytes 122912 | tf_op jit(solution)/shard_map/ppermute | solution.py:160
  80.4 0.7 collective-permute-done.9
  81.5 1.6 %collective-permute-start.12 = (s16[2,240,128]{2,1,0:T(8,128)(2,1)S(1)}, s16[2,240,128]{2,1,0:T(8,128)(2,1)S(1)}, u32[]{:S(2)}, u32[]{:S(2)}) collective-permute-start(s16[2,240,128]{2,1,0:T(8,128)(2,1)S(1)} %add_add_fusion.4), channel_id=1, source_target_pairs={{0,8},{8,0},{16,24},{24,16},{1,9},{9,1},{17,25},{25,17},{2,10},{10... | collective-permute-start | bytes 368648 | tf_op jit(solution)/shard_map/ppermute | solution.py:160
  83.1 3.3 %collective-permute-done.12 = s16[2,240,128]{2,1,0:T(8,128)(2,1)S(1)} collective-permute-done((s16[2,240,128]{2,1,0:T(8,128)(2,1)S(1)}, s16[2,240,128]{2,1,0:T(8,128)(2,1)S(1)}, u32[]{:S(2)}, u32[]{:S(2)}) %collective-permute-start.12) | collective-permute-done | bytes 122912 | tf_op jit(solution)/shard_map/ppermute | solution.py:160
  86.7 3.3 %collective-permute-start.13 = (s16[1,240,128]{2,1,0:T(8,128)(2,1)S(1)}, s16[1,240,128]{2,1,0:T(8,128)(2,1)S(1)}, u32[]{:S(2)}, u32[]{:S(2)}) collective-permute-start(s16[1,240,128]{2,1,0:T(8,128)(2,1)S(1)} %add_add_fusion.5), channel_id=1, source_target_pairs={{0,16},{8,24},{16,0},{24,8},{1,17},{9,25},{17,1},{25,9},{2,18},{10... | collective-permute-start | bytes 184328 | tf_op jit(solution)/shard_map/ppermute | solution.py:160
  90.0 2.2 %collective-permute-done.13 = s16[1,240,128]{2,1,0:T(8,128)(2,1)S(1)} collective-permute-done((s16[1,240,128]{2,1,0:T(8,128)(2,1)S(1)}, s16[1,240,128]{2,1,0:T(8,128)(2,1)S(1)}, u32[]{:S(2)}, u32[]{:S(2)}) %collective-permute-start.13) | collective-permute-done | bytes 61472 | tf_op jit(solution)/shard_map/ppermute | solution.py:160
  92.3 0.7 copy_bitcast_fusion
  (52 shorter events, 2.4 us)
Async XLA Ops:
  0.0 7.2 %collective-permute-start = (bf16[128,512]{1,0:T(8,128)(2,1)}, bf16[128,512]{1,0:T(8,128)(2,1)S(1)}, u32[]{:S(2)}, u32[]{:S(2)}) collective-permute-start(bf16[128,512]{1,0:T(8,128)(2,1)} %refs_0_.1), channel_id=1, source_target_pairs={{0,2},{1,3},{2,0},{3,1},{4,6},{5,7},{6,4},{7,5},{8,10},{9,11},{10,... | collective-permute-start | bytes 393224 | tf_op jit(solution)/shard_map/ppermute | solution.py:160
  2.9 8.0 %collective-permute-start.1 = (bf16[128,512]{1,0:T(8,128)(2,1)}, bf16[128,512]{1,0:T(8,128)(2,1)S(1)}, u32[]{:S(2)}, u32[]{:S(2)}) collective-permute-start(bf16[128,512]{1,0:T(8,128)(2,1)} %refs_0_.1), channel_id=1, source_target_pairs={{0,4},{1,5},{2,6},{3,7},{4,0},{5,1},{6,2},{7,3},{8,12},{9,13},{10,... | collective-permute-start | bytes 393224 | tf_op jit(solution)/shard_map/ppermute | solution.py:160
  4.5 6.5 %collective-permute-start.2 = (bf16[128,512]{1,0:T(8,128)(2,1)}, bf16[128,512]{1,0:T(8,128)(2,1)S(1)}, u32[]{:S(2)}, u32[]{:S(2)}) collective-permute-start(bf16[128,512]{1,0:T(8,128)(2,1)} %refs_0_.1), channel_id=1, source_target_pairs={{0,6},{1,7},{2,4},{3,5},{4,2},{5,3},{6,0},{7,1},{8,14},{9,15},{10,... | collective-permute-start | bytes 393224 | tf_op jit(solution)/shard_map/ppermute | solution.py:160
  4.5 7.7 %collective-permute-start.3 = (bf16[128,512]{1,0:T(8,128)(2,1)}, bf16[128,512]{1,0:T(8,128)(2,1)S(1)}, u32[]{:S(2)}, u32[]{:S(2)}) collective-permute-start(bf16[128,512]{1,0:T(8,128)(2,1)} %refs_0_.1), channel_id=1, source_target_pairs={{0,1},{1,0},{2,3},{3,2},{4,5},{5,4},{6,7},{7,6},{8,9},{9,8},{10,11... | collective-permute-start | bytes 393224 | tf_op jit(solution)/shard_map/ppermute | solution.py:160
  10.9 1.3 %collective-permute-start.4 = (bf16[128,512]{1,0:T(8,128)(2,1)S(1)}, bf16[128,512]{1,0:T(8,128)(2,1)S(1)}, u32[]{:S(2)}, u32[]{:S(2)}) collective-permute-start(bf16[128,512]{1,0:T(8,128)(2,1)S(1)} %collective-permute-done.refs_2_), channel_id=1, source_target_pairs={{0,1},{1,0},{2,3},{3,2},{4,5},{5,4},{6,7},{7,6},{8,9},{9,8},{10,11... | collective-permute-start | bytes 393224 | tf_op jit(solution)/shard_map/ppermute | solution.py:160
  10.9 1.5 %collective-permute-start.5 = (bf16[128,512]{1,0:T(8,128)(2,1)S(1)}, bf16[128,512]{1,0:T(8,128)(2,1)S(1)}, u32[]{:S(2)}, u32[]{:S(2)}) collective-permute-start(bf16[128,512]{1,0:T(8,128)(2,1)S(1)} %collective-permute-done.1.refs_4_), channel_id=1, source_target_pairs={{0,1},{1,0},{2,3},{3,2},{4,5},{5,4},{6,7},{7,6},{8,9},{9,8},{10,11... | collective-permute-start | bytes 393224 | tf_op jit(solution)/shard_map/ppermute | solution.py:160
  11.4 1.3 %collective-permute-start.6 = (bf16[128,512]{1,0:T(8,128)(2,1)S(1)}, bf16[128,512]{1,0:T(8,128)(2,1)S(1)}, u32[]{:S(2)}, u32[]{:S(2)}) collective-permute-start(bf16[128,512]{1,0:T(8,128)(2,1)S(1)} %collective-permute-done.2.refs_6_), channel_id=1, source_target_pairs={{0,1},{1,0},{2,3},{3,2},{4,5},{5,4},{6,7},{7,6},{8,9},{9,8},{10,11... | collective-permute-start | bytes 393224 | tf_op jit(solution)/shard_map/ppermute | solution.py:160
  12.8 0.9 copy-start
  61.0 3.9 %collective-permute-start.7 = (f32[4,4,7,32,128]{4,3,2,1,0:T(8,128)S(1)}, f32[4,4,7,32,128]{4,3,2,1,0:T(8,128)S(1)}, u32[]{:S(2)}, u32[]{:S(2)}) collective-permute-start(f32[4,4,7,32,128]{4,3,2,1,0:T(8,128)S(1)} %get-tuple-element.16), channel_id=1, source_target_pairs={{0,1},{1,0},{2,3},{3,2},{4,5},{5,4},{6,7},{7,6},{8,9},{9,8},{10,11... | collective-permute-start | bytes 5505032 | tf_op jit(solution)/shard_map/ppermute | solution.py:160
  65.9 8.1 %collective-permute-start.8 = (s16[2,2,240,128]{3,2,1,0:T(8,128)(2,1)S(1)}, s16[2,2,240,128]{3,2,1,0:T(8,128)(2,1)S(1)}, u32[]{:S(2)}, u32[]{:S(2)}) collective-permute-start(s16[2,2,240,128]{3,2,1,0:T(8,128)(2,1)S(1)} %get-tuple-element.37), channel_id=1, source_target_pairs={{0,2},{1,3},{2,0},{3,1},{4,6},{5,7},{6,4},{7,5},{8,10},{9,11},{10,... | collective-permute-start | bytes 737288 | tf_op jit(solution)/shard_map/ppermute | solution.py:160
  67.2 7.8 %collective-permute-start.10 = (s16[2,2,240,128]{3,2,1,0:T(8,128)(2,1)S(1)}, s16[2,2,240,128]{3,2,1,0:T(8,128)(2,1)S(1)}, u32[]{:S(2)}, u32[]{:S(2)}) collective-permute-start(s16[2,2,240,128]{3,2,1,0:T(8,128)(2,1)S(1)} %get-tuple-element.38), channel_id=1, source_target_pairs={{0,4},{1,5},{2,6},{3,7},{4,0},{5,1},{6,2},{7,3},{8,12},{9,13},{10,... | collective-permute-start | bytes 737288 | tf_op jit(solution)/shard_map/ppermute | solution.py:160
  75.4 4.9 %collective-permute-start.11 = (s16[2,240,128]{2,1,0:T(8,128)(2,1)S(1)}, s16[2,240,128]{2,1,0:T(8,128)(2,1)S(1)}, u32[]{:S(2)}, u32[]{:S(2)}) collective-permute-start(s16[2,240,128]{2,1,0:T(8,128)(2,1)S(1)} %get-tuple-element.36), channel_id=1, source_target_pairs={{0,2},{1,3},{2,0},{3,1},{4,6},{5,7},{6,4},{7,5},{8,10},{9,11},{10,... | collective-permute-start | bytes 368648 | tf_op jit(solution)/shard_map/ppermute | solution.py:160
  76.3 4.9 %collective-permute-start.9 = (s16[2,240,128]{2,1,0:T(8,128)(2,1)S(1)}, s16[2,240,128]{2,1,0:T(8,128)(2,1)S(1)}, u32[]{:S(2)}, u32[]{:S(2)}) collective-permute-start(s16[2,240,128]{2,1,0:T(8,128)(2,1)S(1)} %get-tuple-element.35), channel_id=1, source_target_pairs={{0,4},{1,5},{2,6},{3,7},{4,0},{5,1},{6,2},{7,3},{8,12},{9,13},{10,... | collective-permute-start | bytes 368648 | tf_op jit(solution)/shard_map/ppermute | solution.py:160
  81.5 4.9 %collective-permute-start.12 = (s16[2,240,128]{2,1,0:T(8,128)(2,1)S(1)}, s16[2,240,128]{2,1,0:T(8,128)(2,1)S(1)}, u32[]{:S(2)}, u32[]{:S(2)}) collective-permute-start(s16[2,240,128]{2,1,0:T(8,128)(2,1)S(1)} %add_add_fusion.4), channel_id=1, source_target_pairs={{0,8},{8,0},{16,24},{24,16},{1,9},{9,1},{17,25},{25,17},{2,10},{10... | collective-permute-start | bytes 368648 | tf_op jit(solution)/shard_map/ppermute | solution.py:160
  86.7 5.5 %collective-permute-start.13 = (s16[1,240,128]{2,1,0:T(8,128)(2,1)S(1)}, s16[1,240,128]{2,1,0:T(8,128)(2,1)S(1)}, u32[]{:S(2)}, u32[]{:S(2)}) collective-permute-start(s16[1,240,128]{2,1,0:T(8,128)(2,1)S(1)} %add_add_fusion.5), channel_id=1, source_target_pairs={{0,16},{8,24},{16,0},{24,8},{1,17},{9,25},{17,1},{25,9},{2,18},{10... | collective-permute-start | bytes 184328 | tf_op jit(solution)/shard_map/ppermute | solution.py:160

commit v4 on v3

--- a/solution.py
+++ b/solution.py
@@ -99,6 +99,7 @@
     sizes = (aux_blocks, span, depth, edge, width, slots, groups)
     part = (slots // 2, groups, offsets, edge // groups, edge)
     anywhere = pl.BlockSpec(memory_space=pl.ANY)
+    in_place = pl.BlockSpec(memory_space=pltpu.HBM)
     scalars = pl.BlockSpec(memory_space=pltpu.SMEM)
     buffers = [
         pltpu.VMEM((slots, edge, width), jnp.bfloat16),
@@ -113,7 +114,7 @@
     return pl.pallas_call(
         functools.partial(band_kernel, sizes),
         out_shape=[jax.ShapeDtypeStruct(part, jnp.float32)] * 2,
-        in_specs=[scalars] + [anywhere] * (slots + 1),
+        in_specs=[scalars, in_place] + [anywhere] * (slots - 1) + [in_place],
         out_specs=[anywhere] * 2,
         scratch_shapes=buffers
         + [
@@ -165,9 +166,8 @@
     slots = {0: occupied, 1: swap(occupied, "orb", 1)}
     for s in range(2, orb_size, 2):
         slots[s] = swap(occupied, "orb", s)
-    arrived, block_lists = lax.optimization_barrier(([slots[s] for s in range(2, orb_size, 2)], block_lists + 0))
+    slots[2], block_lists = lax.optimization_barrier((slots[2], block_lists + 0))
     for s in range(2, orb_size, 2):
-        slots[s] = arrived[s // 2 - 1]
         slots[s + 1] = swap(slots[s], "orb", 1)
     keep, send = band_partials(block_lists, [slots[s] for s in range(orb_size)], three_centre, aux_size)
 
@@ -185,10 +185,7 @@
             left.remove(bit)
         halves.append(taken)
     rows = jnp.concatenate(halves, axis=0)
-    step = 1
-    while step < aux_size:
-        rows = rows[0::2] + swap_sums(rows[1::2], "aux", step)
-        step *= 2
+    rows = sum((swap_sums(rows[g : g + 1], "aux", g) for g in range(1, aux_size)), rows[:1])
     return jnp.transpose(rows, (0, 2, 1, 3)).reshape(1, rows.shape[2], rows.shape[1] * rows.shape[3])
 
 

time: 93.1 us -> 91 us (0.977)
  starting transfers between devices: 14.7 us -> 13.4 us
    ppermute x14 -> x15, starting transfers between devices: 14.7 us -> 13.4 us  [swap(): return lax.ppermute(value, axis, [(i, i ^ bits) for i in range(size)])]
    ppermute x14 -> x15, waiting for transfers between devices: 26.1 us -> 25.4 us  [swap(): return lax.ppermute(value, axis, [(i, i ^ bits) for i in range(size)])]
  transfers between devices with their start and end apart: 14 -> 15, of which waited for: 12 -> 11; matrix products, arithmetic and copies ran while one was open for 1% -> 1% of each run, Pallas kernels for 0% -> 0%
where the time goes in v4:
time: 91 us; the launch traced here: 90.9 us
  Pallas kernels  47.3 us (52%)
  waiting for transfers between devices  25.4 us (28%)
  starting transfers between devices  13.4 us (15%)
  other arithmetic  2.62 us (3%)
  local copies, waits for them, and re-layouts  1.87 us (2%)
    pallas_call x1, Pallas kernels, band_partials(): pl.pallas_call(functools.partial(band_kernel, sizes), out_shape=[jax.Shap...  47.3 us
    ppermute x15, waiting for transfers between devices, swap(): return lax.ppermute(value, axis, [(i, i ^ bits) for i in range(size)])  25.4 us
    ppermute x15, starting transfers between devices, swap(): return lax.ppermute(value, axis, [(i, i ^ bits) for i in range(size)])  13.4 us
  transfers between devices with their start and end apart: 15, of which 11 were waited for; matrix products, arithmetic and copies ran while one was open for 1% of the time, Pallas kernels for 0%

profile of v4, /device:TPU:0, one launch (start us, length us, event | category | flops | bytes accessed | tf_op | source)
XLA Modules:
  0.0 90.9 jit_solution(994068716145177304)
XLA Ops:
  0.0 2.9 %collective-permute-start = (bf16[128,512]{1,0:T(8,128)(2,1)}, bf16[128,512]{1,0:T(8,128)(2,1)S(1)}, u32[]{:S(2)}, u32[]{:S(2)}) collective-permute-start(bf16[128,512]{1,0:T(8,128)(2,1)} %refs_0_.1), channel_id=1, source_target_pairs={{0,2},{1,3},{2,0},{3,1},{4,6},{5,7},{6,4},{7,5},{8,10},{9,11},{10,... | collective-permute-start | bytes 393224 | tf_op jit(solution)/shard_map/ppermute | solution.py:161
  2.9 1.5 %collective-permute-start.3 = (bf16[128,512]{1,0:T(8,128)(2,1)}, bf16[128,512]{1,0:T(8,128)(2,1)S(1)}, u32[]{:S(2)}, u32[]{:S(2)}) collective-permute-start(bf16[128,512]{1,0:T(8,128)(2,1)} %refs_0_.1), channel_id=1, source_target_pairs={{0,4},{1,5},{2,6},{3,7},{4,0},{5,1},{6,2},{7,3},{8,12},{9,13},{10,... | collective-permute-start | bytes 393224 | tf_op jit(solution)/shard_map/ppermute | solution.py:161
  4.5 2.7 %collective-permute-done.refs_2_ = bf16[128,512]{1,0:T(8,128)(2,1)S(1)} collective-permute-done((bf16[128,512]{1,0:T(8,128)(2,1)}, bf16[128,512]{1,0:T(8,128)(2,1)S(1)}, u32[]{:S(2)}, u32[]{:S(2)}) %collective-permute-start) | collective-permute-done | bytes 131104 | tf_op jit(solution)/shard_map/ppermute | solution.py:161
  7.2 3.8 %collective-permute-done.3.refs_4_ = bf16[128,512]{1,0:T(8,128)(2,1)S(1)} collective-permute-done((bf16[128,512]{1,0:T(8,128)(2,1)}, bf16[128,512]{1,0:T(8,128)(2,1)S(1)}, u32[]{:S(2)}, u32[]{:S(2)}) %collective-permute-start.3) | collective-permute-done | bytes 131104 | tf_op jit(solution)/shard_map/ppermute | solution.py:161
  10.9 0.5 collective-permute-start.6
  11.4 0.8 copy.5.lists_ref
  12.5 0.9 copy-done
  13.4 47.3 %band_partials.1 = (f32[4,4,7,32,128]{4,3,2,1,0:T(8,128)S(1)}, f32[4,4,7,32,128]{4,3,2,1,0:T(8,128)S(1)}) custom-call(s32[8,3]{1,0:T(8,128)S(1)} %copy.5.lists_ref, bf16[128,512]{1,0:T(8,128)(2,1)S(1)} %copy-done, bf16[128,512]{1,0:T(8,128)(2,1)S(1)} %collective-permute-done.1.refs_1_, bf16[128,512]{1,0:T(8,128)(2,1)S(1)} %collective-permute-done.refs_2_, ...), custom_call_target="tpu_custom_call" | custom-call | tf_op jit(solution)/shard_map/band_partials/pallas_call | solution.py:114
  60.7 0.4 collective-permute-start.7
  61.2 3.4 %collective-permute-done.7 = f32[4,4,7,32,128]{4,3,2,1,0:T(8,128)S(1)} collective-permute-done((f32[4,4,7,32,128]{4,3,2,1,0:T(8,128)S(1)}, f32[4,4,7,32,128]{4,3,2,1,0:T(8,128)S(1)}, u32[]{:S(2)}, u32[]{:S(2)}) %collective-permute-start.7) | collective-permute-done | bytes 1835040 | tf_op jit(solution)/shard_map/ppermute | solution.py:161
  64.6 0.4 add.195
  65.6 1.6 %collective-permute-start.11 = (s16[2,2,240,128]{3,2,1,0:T(8,128)(2,1)S(1)}, s16[2,2,240,128]{3,2,1,0:T(8,128)(2,1)S(1)}, u32[]{:S(2)}, u32[]{:S(2)}) collective-permute-start(s16[2,2,240,128]{3,2,1,0:T(8,128)(2,1)S(1)} %get-tuple-element.42), channel_id=1, source_target_pairs={{0,4},{1,5},{2,6},{3,7},{4,0},{5,1},{6,2},{7,3},{8,12},{9,13},{10,... | collective-permute-start | bytes 737288 | tf_op jit(solution)/shard_map/ppermute | solution.py:161
  67.2 0.5 collective-permute-start.8
  67.7 6.1 %collective-permute-done.11 = s16[2,2,240,128]{3,2,1,0:T(8,128)(2,1)S(1)} collective-permute-done((s16[2,2,240,128]{3,2,1,0:T(8,128)(2,1)S(1)}, s16[2,2,240,128]{3,2,1,0:T(8,128)(2,1)S(1)}, u32[]{:S(2)}, u32[]{:S(2)}) %collective-permute-start.11) | collective-permute-done | bytes 245792 | tf_op jit(solution)/shard_map/ppermute | solution.py:161
  74.1 1.0 %collective-permute-done.8 = s16[2,2,240,128]{3,2,1,0:T(8,128)(2,1)S(1)} collective-permute-done((s16[2,2,240,128]{3,2,1,0:T(8,128)(2,1)S(1)}, s16[2,2,240,128]{3,2,1,0:T(8,128)(2,1)S(1)}, u32[]{:S(2)}, u32[]{:S(2)}) %collective-permute-start.8) | collective-permute-done | bytes 245792 | tf_op jit(solution)/shard_map/ppermute | solution.py:161
  75.5 0.6 collective-permute-start.9
  76.1 0.9 collective-permute-start.12
  76.9 3.5 %collective-permute-done.9 = s16[2,240,128]{2,1,0:T(8,128)(2,1)S(1)} collective-permute-done((s16[2,240,128]{2,1,0:T(8,128)(2,1)S(1)}, s16[2,240,128]{2,1,0:T(8,128)(2,1)S(1)}, u32[]{:S(2)}, u32[]{:S(2)}) %collective-permute-start.9) | collective-permute-done | bytes 122912 | tf_op jit(solution)/shard_map/ppermute | solution.py:161
  80.6 0.4 collective-permute-done.12
  81.3 3.7 %collective-permute-start.14 = (s16[1,240,128]{2,1,0:T(8,128)(2,1)S(1)}, s16[1,240,128]{2,1,0:T(8,128)(2,1)S(1)}, u32[]{:S(2)}, u32[]{:S(2)}) collective-permute-start(s16[1,240,128]{2,1,0:T(8,128)(2,1)S(1)} %get-tuple-element.39), channel_id=1, source_target_pairs={{0,24},{8,16},{16,8},{24,0},{1,25},{9,17},{17,9},{25,1},{2,26},{10... | collective-permute-start | bytes 184328 | tf_op jit(solution)/shard_map/ppermute | solution.py:161
  85.0 0.8 collective-permute-start.10
  85.8 1.7 %collective-permute-done.14 = s16[1,240,128]{2,1,0:T(8,128)(2,1)S(1)} collective-permute-done((s16[1,240,128]{2,1,0:T(8,128)(2,1)S(1)}, s16[1,240,128]{2,1,0:T(8,128)(2,1)S(1)}, u32[]{:S(2)}, u32[]{:S(2)}) %collective-permute-start.14) | collective-permute-done | bytes 61472 | tf_op jit(solution)/shard_map/ppermute | solution.py:161
  87.5 2.6 %collective-permute-done.13 = s16[1,240,128]{2,1,0:T(8,128)(2,1)S(1)} collective-permute-done((s16[1,240,128]{2,1,0:T(8,128)(2,1)S(1)}, s16[1,240,128]{2,1,0:T(8,128)(2,1)S(1)}, u32[]{:S(2)}, u32[]{:S(2)}) %collective-permute-start.13) | collective-permute-done | bytes 61472 | tf_op jit(solution)/shard_map/ppermute | solution.py:161
  90.2 0.7 copy_bitcast_fusion
  (54 shorter events, 2.0 us)
Async XLA Ops:
  0.0 7.2 %collective-permute-start = (bf16[128,512]{1,0:T(8,128)(2,1)}, bf16[128,512]{1,0:T(8,128)(2,1)S(1)}, u32[]{:S(2)}, u32[]{:S(2)}) collective-permute-start(bf16[128,512]{1,0:T(8,128)(2,1)} %refs_0_.1), channel_id=1, source_target_pairs={{0,2},{1,3},{2,0},{3,1},{4,6},{5,7},{6,4},{7,5},{8,10},{9,11},{10,... | collective-permute-start | bytes 393224 | tf_op jit(solution)/shard_map/ppermute | solution.py:161
  2.9 8.0 %collective-permute-start.3 = (bf16[128,512]{1,0:T(8,128)(2,1)}, bf16[128,512]{1,0:T(8,128)(2,1)S(1)}, u32[]{:S(2)}, u32[]{:S(2)}) collective-permute-start(bf16[128,512]{1,0:T(8,128)(2,1)} %refs_0_.1), channel_id=1, source_target_pairs={{0,4},{1,5},{2,6},{3,7},{4,0},{5,1},{6,2},{7,3},{8,12},{9,13},{10,... | collective-permute-start | bytes 393224 | tf_op jit(solution)/shard_map/ppermute | solution.py:161
  4.5 6.5 %collective-permute-start.5 = (bf16[128,512]{1,0:T(8,128)(2,1)}, bf16[128,512]{1,0:T(8,128)(2,1)S(1)}, u32[]{:S(2)}, u32[]{:S(2)}) collective-permute-start(bf16[128,512]{1,0:T(8,128)(2,1)} %refs_0_.1), channel_id=1, source_target_pairs={{0,6},{1,7},{2,4},{3,5},{4,2},{5,3},{6,0},{7,1},{8,14},{9,15},{10,... | collective-permute-start | bytes 393224 | tf_op jit(solution)/shard_map/ppermute | solution.py:161
  4.5 7.7 %collective-permute-start.1 = (bf16[128,512]{1,0:T(8,128)(2,1)}, bf16[128,512]{1,0:T(8,128)(2,1)S(1)}, u32[]{:S(2)}, u32[]{:S(2)}) collective-permute-start(bf16[128,512]{1,0:T(8,128)(2,1)} %refs_0_.1), channel_id=1, source_target_pairs={{0,1},{1,0},{2,3},{3,2},{4,5},{5,4},{6,7},{7,6},{8,9},{9,8},{10,11... | collective-permute-start | bytes 393224 | tf_op jit(solution)/shard_map/ppermute | solution.py:161
  7.2 5.0 %collective-permute-start.2 = (bf16[128,512]{1,0:T(8,128)(2,1)S(1)}, bf16[128,512]{1,0:T(8,128)(2,1)S(1)}, u32[]{:S(2)}, u32[]{:S(2)}) collective-permute-start(bf16[128,512]{1,0:T(8,128)(2,1)S(1)} %collective-permute-done.refs_2_), channel_id=1, source_target_pairs={{0,1},{1,0},{2,3},{3,2},{4,5},{5,4},{6,7},{7,6},{8,9},{9,8},{10,11... | collective-permute-start | bytes 393224 | tf_op jit(solution)/shard_map/ppermute | solution.py:161
  10.9 1.3 %collective-permute-start.4 = (bf16[128,512]{1,0:T(8,128)(2,1)S(1)}, bf16[128,512]{1,0:T(8,128)(2,1)S(1)}, u32[]{:S(2)}, u32[]{:S(2)}) collective-permute-start(bf16[128,512]{1,0:T(8,128)(2,1)S(1)} %collective-permute-done.3.refs_4_), channel_id=1, source_target_pairs={{0,1},{1,0},{2,3},{3,2},{4,5},{5,4},{6,7},{7,6},{8,9},{9,8},{10,11... | collective-permute-start | bytes 393224 | tf_op jit(solution)/shard_map/ppermute | solution.py:161
  10.9 1.5 %collective-permute-start.6 = (bf16[128,512]{1,0:T(8,128)(2,1)S(1)}, bf16[128,512]{1,0:T(8,128)(2,1)S(1)}, u32[]{:S(2)}, u32[]{:S(2)}) collective-permute-start(bf16[128,512]{1,0:T(8,128)(2,1)S(1)} %collective-permute-done.5.refs_6_), channel_id=1, source_target_pairs={{0,1},{1,0},{2,3},{3,2},{4,5},{5,4},{6,7},{7,6},{8,9},{9,8},{10,11... | collective-permute-start | bytes 393224 | tf_op jit(solution)/shard_map/ppermute | solution.py:161
  12.5 0.9 copy-start
  60.7 3.9 %collective-permute-start.7 = (f32[4,4,7,32,128]{4,3,2,1,0:T(8,128)S(1)}, f32[4,4,7,32,128]{4,3,2,1,0:T(8,128)S(1)}, u32[]{:S(2)}, u32[]{:S(2)}) collective-permute-start(f32[4,4,7,32,128]{4,3,2,1,0:T(8,128)S(1)} %get-tuple-element.12), channel_id=1, source_target_pairs={{0,1},{1,0},{2,3},{3,2},{4,5},{5,4},{6,7},{7,6},{8,9},{9,8},{10,11... | collective-permute-start | bytes 5505032 | tf_op jit(solution)/shard_map/ppermute | solution.py:161
  65.6 8.2 %collective-permute-start.11 = (s16[2,2,240,128]{3,2,1,0:T(8,128)(2,1)S(1)}, s16[2,2,240,128]{3,2,1,0:T(8,128)(2,1)S(1)}, u32[]{:S(2)}, u32[]{:S(2)}) collective-permute-start(s16[2,2,240,128]{3,2,1,0:T(8,128)(2,1)S(1)} %get-tuple-element.42), channel_id=1, source_target_pairs={{0,4},{1,5},{2,6},{3,7},{4,0},{5,1},{6,2},{7,3},{8,12},{9,13},{10,... | collective-permute-start | bytes 737288 | tf_op jit(solution)/shard_map/ppermute | solution.py:161
  67.2 7.9 %collective-permute-start.8 = (s16[2,2,240,128]{3,2,1,0:T(8,128)(2,1)S(1)}, s16[2,2,240,128]{3,2,1,0:T(8,128)(2,1)S(1)}, u32[]{:S(2)}, u32[]{:S(2)}) collective-permute-start(s16[2,2,240,128]{3,2,1,0:T(8,128)(2,1)S(1)} %get-tuple-element.43), channel_id=1, source_target_pairs={{0,2},{1,3},{2,0},{3,1},{4,6},{5,7},{6,4},{7,5},{8,10},{9,11},{10,... | collective-permute-start | bytes 737288 | tf_op jit(solution)/shard_map/ppermute | solution.py:161
  75.5 4.9 %collective-permute-start.9 = (s16[2,240,128]{2,1,0:T(8,128)(2,1)S(1)}, s16[2,240,128]{2,1,0:T(8,128)(2,1)S(1)}, u32[]{:S(2)}, u32[]{:S(2)}) collective-permute-start(s16[2,240,128]{2,1,0:T(8,128)(2,1)S(1)} %get-tuple-element.41), channel_id=1, source_target_pairs={{0,4},{1,5},{2,6},{3,7},{4,0},{5,1},{6,2},{7,3},{8,12},{9,13},{10,... | collective-permute-start | bytes 368648 | tf_op jit(solution)/shard_map/ppermute | solution.py:161
  76.1 4.9 %collective-permute-start.12 = (s16[2,240,128]{2,1,0:T(8,128)(2,1)S(1)}, s16[2,240,128]{2,1,0:T(8,128)(2,1)S(1)}, u32[]{:S(2)}, u32[]{:S(2)}) collective-permute-start(s16[2,240,128]{2,1,0:T(8,128)(2,1)S(1)} %get-tuple-element.40), channel_id=1, source_target_pairs={{0,2},{1,3},{2,0},{3,1},{4,6},{5,7},{6,4},{7,5},{8,10},{9,11},{10,... | collective-permute-start | bytes 368648 | tf_op jit(solution)/shard_map/ppermute | solution.py:161
  81.3 6.2 %collective-permute-start.14 = (s16[1,240,128]{2,1,0:T(8,128)(2,1)S(1)}, s16[1,240,128]{2,1,0:T(8,128)(2,1)S(1)}, u32[]{:S(2)}, u32[]{:S(2)}) collective-permute-start(s16[1,240,128]{2,1,0:T(8,128)(2,1)S(1)} %get-tuple-element.39), channel_id=1, source_target_pairs={{0,24},{8,16},{16,8},{24,0},{1,25},{9,17},{17,9},{25,1},{2,26},{10... | collective-permute-start | bytes 184328 | tf_op jit(solution)/shard_map/ppermute | solution.py:161
  85.0 5.1 %collective-permute-start.13 = (s16[1,240,128]{2,1,0:T(8,128)(2,1)S(1)}, s16[1,240,128]{2,1,0:T(8,128)(2,1)S(1)}, u32[]{:S(2)}, u32[]{:S(2)}) collective-permute-start(s16[1,240,128]{2,1,0:T(8,128)(2,1)S(1)} %get-tuple-element.38), channel_id=1, source_target_pairs={{0,16},{8,24},{16,0},{24,8},{1,17},{9,25},{17,1},{25,9},{2,18},{10... | collective-permute-start | bytes 184328 | tf_op jit(solution)/shard_map/ppermute | solution.py:161
  85.0 5.2 %collective-permute-start.10 = (s16[1,240,128]{2,1,0:T(8,128)(2,1)S(1)}, s16[1,240,128]{2,1,0:T(8,128)(2,1)S(1)}, u32[]{:S(2)}, u32[]{:S(2)}) collective-permute-start(s16[1,240,128]{2,1,0:T(8,128)(2,1)S(1)} %get-tuple-element.37), channel_id=1, source_target_pairs={{0,8},{8,0},{16,24},{24,16},{1,9},{9,1},{17,25},{25,17},{2,10},{10... | collective-permute-start | bytes 184328 | tf_op jit(solution)/shard_map/ppermute | solution.py:161

commit v5 on v4

--- a/solution.py
+++ b/solution.py
@@ -13,7 +13,7 @@
     aux_blocks, span, depth, edge, width, slots, groups = sizes
     coeff_refs, refs = refs[:slots], refs[slots:]
     integrals_ref, keep_ref, send_ref = refs[:3]
-    coeffs, chosen, integrals, half, flipped, total, band, load_sem, coeff_sem, out_sem = refs[3:]
+    coeffs, chosen, integrals, half, flipped, total, band, load_sem, coeff_sem = refs[3:]
     orb, aux = lax.axis_index("orb"), lax.axis_index("aux")
     rows = edge // groups
 
@@ -79,16 +79,10 @@
             def _():
                 band[(row + offset) ^ orb, span - offset] = band[slot, span + offset].T
 
-    outs = []
     for side, ref in enumerate((keep_ref, send_ref)):
         for s in range(slots // 2):
             for g in range(groups):
-                source = band.at[2 * s + side, :, pl.ds(g * rows, rows)]
-                outs.append(pltpu.make_async_copy(source, ref.at[s, g ^ aux], out_sem.at[side, s, g]))
-    for copy in outs:
-        copy.start()
-    for copy in outs:
-        copy.wait()
+                ref[s, g ^ aux] = band[2 * s + side, :, g * rows : (g + 1) * rows]
 
 
 def band_partials(block_lists, coeff_slots, three_centre, groups):
@@ -99,7 +93,6 @@
     sizes = (aux_blocks, span, depth, edge, width, slots, groups)
     part = (slots // 2, groups, offsets, edge // groups, edge)
     anywhere = pl.BlockSpec(memory_space=pl.ANY)
-    in_place = pl.BlockSpec(memory_space=pltpu.HBM)
     scalars = pl.BlockSpec(memory_space=pltpu.SMEM)
     buffers = [
         pltpu.VMEM((slots, edge, width), jnp.bfloat16),
@@ -111,18 +104,18 @@
         pltpu.VMEM((slots, offsets, edge, edge), jnp.float32),
     ]
     held = sum(math.prod(b.shape) * jnp.dtype(b.dtype).itemsize for b in buffers)
+    given = 2 * math.prod(part) * 4
     return pl.pallas_call(
         functools.partial(band_kernel, sizes),
         out_shape=[jax.ShapeDtypeStruct(part, jnp.float32)] * 2,
-        in_specs=[scalars, in_place] + [anywhere] * (slots - 1) + [in_place],
-        out_specs=[anywhere] * 2,
+        in_specs=[scalars] + [anywhere] * (slots + 1),
+        out_specs=[pl.BlockSpec(memory_space=pltpu.VMEM)] * 2,
         scratch_shapes=buffers
         + [
             pltpu.SemaphoreType.DMA((2, span)),
             pltpu.SemaphoreType.DMA((slots,)),
-            pltpu.SemaphoreType.DMA((2, slots // 2, groups)),
         ],
-        compiler_params=pltpu.CompilerParams(vmem_limit_bytes=held + 8 * 2**20),
+        compiler_params=pltpu.CompilerParams(vmem_limit_bytes=held + given + 4 * 2**20),
         name="band_partials",
     )(block_lists, *coeff_slots, three_centre)
 

time: 91 us -> 90.2 us (level)
  no operation moved by 1% of the time
where the time goes in v5:
time: 90.2 us; the launch traced here: 90.1 us
  Pallas kernels  46.5 us (52%)
  waiting for transfers between devices  25.4 us (28%)
  starting transfers between devices  13.4 us (15%)
  other arithmetic  2.62 us (3%)
  local copies, waits for them, and re-layouts  1.87 us (2%)
    pallas_call x1, Pallas kernels, band_partials(): pl.pallas_call(functools.partial(band_kernel, sizes), out_shape=[jax.Shap...  46.5 us
    ppermute x15, waiting for transfers between devices, swap(): return lax.ppermute(value, axis, [(i, i ^ bits) for i in range(size)])  25.4 us
    ppermute x15, starting transfers between devices, swap(): return lax.ppermute(value, axis, [(i, i ^ bits) for i in range(size)])  13.4 us
  transfers between devices with their start and end apart: 15, of which 11 were waited for; matrix products, arithmetic and copies ran while one was open for 1% of the time, Pallas kernels for 0%

profile of v5, /device:TPU:0, one launch (start us, length us, event | category | flops | bytes accessed | tf_op | source)
XLA Modules:
  0.0 90.1 jit_solution(3333546418257161445)
XLA Ops:
  0.0 2.9 %collective-permute-start = (bf16[128,512]{1,0:T(8,128)(2,1)}, bf16[128,512]{1,0:T(8,128)(2,1)S(1)}, u32[]{:S(2)}, u32[]{:S(2)}) collective-permute-start(bf16[128,512]{1,0:T(8,128)(2,1)} %refs_0_.1), channel_id=1, source_target_pairs={{0,2},{1,3},{2,0},{3,1},{4,6},{5,7},{6,4},{7,5},{8,10},{9,11},{10,... | collective-permute-start | bytes 393224 | tf_op jit(solution)/shard_map/ppermute | solution.py:154
  2.9 1.5 %collective-permute-start.3 = (bf16[128,512]{1,0:T(8,128)(2,1)}, bf16[128,512]{1,0:T(8,128)(2,1)S(1)}, u32[]{:S(2)}, u32[]{:S(2)}) collective-permute-start(bf16[128,512]{1,0:T(8,128)(2,1)} %refs_0_.1), channel_id=1, source_target_pairs={{0,4},{1,5},{2,6},{3,7},{4,0},{5,1},{6,2},{7,3},{8,12},{9,13},{10,... | collective-permute-start | bytes 393224 | tf_op jit(solution)/shard_map/ppermute | solution.py:154
  4.5 2.7 %collective-permute-done.refs_2_ = bf16[128,512]{1,0:T(8,128)(2,1)S(1)} collective-permute-done((bf16[128,512]{1,0:T(8,128)(2,1)}, bf16[128,512]{1,0:T(8,128)(2,1)S(1)}, u32[]{:S(2)}, u32[]{:S(2)}) %collective-permute-start) | collective-permute-done | bytes 131104 | tf_op jit(solution)/shard_map/ppermute | solution.py:154
  7.2 3.8 %collective-permute-done.3.refs_4_ = bf16[128,512]{1,0:T(8,128)(2,1)S(1)} collective-permute-done((bf16[128,512]{1,0:T(8,128)(2,1)}, bf16[128,512]{1,0:T(8,128)(2,1)S(1)}, u32[]{:S(2)}, u32[]{:S(2)}) %collective-permute-start.3) | collective-permute-done | bytes 131104 | tf_op jit(solution)/shard_map/ppermute | solution.py:154
  10.9 0.5 collective-permute-start.6
  11.4 0.8 copy.5.lists_ref
  12.5 0.9 %copy-done = bf16[128,512]{1,0:T(8,128)(2,1)S(1)} copy-done((bf16[128,512]{1,0:T(8,128)(2,1)S(1)}, bf16[128,512]{1,0:T(8,128)(2,1)}, u32[]{:S(2)}) %copy-start) | copy-done | bytes 131096
  13.4 46.5 %band_partials.1 = (f32[4,4,7,32,128]{4,3,2,1,0:T(8,128)S(1)}, f32[4,4,7,32,128]{4,3,2,1,0:T(8,128)S(1)}) custom-call(s32[8,3]{1,0:T(8,128)S(1)} %copy.5.lists_ref, bf16[128,512]{1,0:T(8,128)(2,1)S(1)} %copy-done, bf16[128,512]{1,0:T(8,128)(2,1)S(1)} %collective-permute-done.1.refs_1_, bf16[128,512]{1,0:T(8,128)(2,1)S(1)} %collective-permute-done.refs_2_, ...), custom_call_target="tpu_custom_call" | custom-call | tf_op jit(solution)/shard_map/band_partials/pallas_call | solution.py:108
  59.9 0.4 collective-permute-start.7
  60.4 3.4 %collective-permute-done.7 = f32[4,4,7,32,128]{4,3,2,1,0:T(8,128)S(1)} collective-permute-done((f32[4,4,7,32,128]{4,3,2,1,0:T(8,128)S(1)}, f32[4,4,7,32,128]{4,3,2,1,0:T(8,128)S(1)}, u32[]{:S(2)}, u32[]{:S(2)}) %collective-permute-start.7) | collective-permute-done | bytes 1835040 | tf_op jit(solution)/shard_map/ppermute | solution.py:154
  63.8 0.4 add.195
  64.8 1.6 %collective-permute-start.11 = (s16[2,2,240,128]{3,2,1,0:T(8,128)(2,1)S(1)}, s16[2,2,240,128]{3,2,1,0:T(8,128)(2,1)S(1)}, u32[]{:S(2)}, u32[]{:S(2)}) collective-permute-start(s16[2,2,240,128]{3,2,1,0:T(8,128)(2,1)S(1)} %get-tuple-element.42), channel_id=1, source_target_pairs={{0,4},{1,5},{2,6},{3,7},{4,0},{5,1},{6,2},{7,3},{8,12},{9,13},{10,... | collective-permute-start | bytes 737288 | tf_op jit(solution)/shard_map/ppermute | solution.py:154
  66.4 0.5 collective-permute-start.8
  66.9 6.1 %collective-permute-done.11 = s16[2,2,240,128]{3,2,1,0:T(8,128)(2,1)S(1)} collective-permute-done((s16[2,2,240,128]{3,2,1,0:T(8,128)(2,1)S(1)}, s16[2,2,240,128]{3,2,1,0:T(8,128)(2,1)S(1)}, u32[]{:S(2)}, u32[]{:S(2)}) %collective-permute-start.11) | collective-permute-done | bytes 245792 | tf_op jit(solution)/shard_map/ppermute | solution.py:154
  73.3 1.0 %collective-permute-done.8 = s16[2,2,240,128]{3,2,1,0:T(8,128)(2,1)S(1)} collective-permute-done((s16[2,2,240,128]{3,2,1,0:T(8,128)(2,1)S(1)}, s16[2,2,240,128]{3,2,1,0:T(8,128)(2,1)S(1)}, u32[]{:S(2)}, u32[]{:S(2)}) %collective-permute-start.8) | collective-permute-done | bytes 245792 | tf_op jit(solution)/shard_map/ppermute | solution.py:154
  74.7 0.6 collective-permute-start.9
  75.3 0.9 collective-permute-start.12
  76.1 3.5 %collective-permute-done.9 = s16[2,240,128]{2,1,0:T(8,128)(2,1)S(1)} collective-permute-done((s16[2,240,128]{2,1,0:T(8,128)(2,1)S(1)}, s16[2,240,128]{2,1,0:T(8,128)(2,1)S(1)}, u32[]{:S(2)}, u32[]{:S(2)}) %collective-permute-start.9) | collective-permute-done | bytes 122912 | tf_op jit(solution)/shard_map/ppermute | solution.py:154
  79.8 0.3 collective-permute-done.12
  80.5 3.7 %collective-permute-start.14 = (s16[1,240,128]{2,1,0:T(8,128)(2,1)S(1)}, s16[1,240,128]{2,1,0:T(8,128)(2,1)S(1)}, u32[]{:S(2)}, u32[]{:S(2)}) collective-permute-start(s16[1,240,128]{2,1,0:T(8,128)(2,1)S(1)} %get-tuple-element.39), channel_id=1, source_target_pairs={{0,24},{8,16},{16,8},{24,0},{1,25},{9,17},{17,9},{25,1},{2,26},{10... | collective-permute-start | bytes 184328 | tf_op jit(solution)/shard_map/ppermute | solution.py:154
  84.2 0.8 collective-permute-start.10
  85.0 1.7 %collective-permute-done.14 = s16[1,240,128]{2,1,0:T(8,128)(2,1)S(1)} collective-permute-done((s16[1,240,128]{2,1,0:T(8,128)(2,1)S(1)}, s16[1,240,128]{2,1,0:T(8,128)(2,1)S(1)}, u32[]{:S(2)}, u32[]{:S(2)}) %collective-permute-start.14) | collective-permute-done | bytes 61472 | tf_op jit(solution)/shard_map/ppermute | solution.py:154
  86.7 2.6 %collective-permute-done.13 = s16[1,240,128]{2,1,0:T(8,128)(2,1)S(1)} collective-permute-done((s16[1,240,128]{2,1,0:T(8,128)(2,1)S(1)}, s16[1,240,128]{2,1,0:T(8,128)(2,1)S(1)}, u32[]{:S(2)}, u32[]{:S(2)}) %collective-permute-start.13) | collective-permute-done | bytes 61472 | tf_op jit(solution)/shard_map/ppermute | solution.py:154
  89.4 0.7 copy_bitcast_fusion
  (54 shorter events, 2.0 us)
Async XLA Ops:
  0.0 7.2 %collective-permute-start = (bf16[128,512]{1,0:T(8,128)(2,1)}, bf16[128,512]{1,0:T(8,128)(2,1)S(1)}, u32[]{:S(2)}, u32[]{:S(2)}) collective-permute-start(bf16[128,512]{1,0:T(8,128)(2,1)} %refs_0_.1), channel_id=1, source_target_pairs={{0,2},{1,3},{2,0},{3,1},{4,6},{5,7},{6,4},{7,5},{8,10},{9,11},{10,... | collective-permute-start | bytes 393224 | tf_op jit(solution)/shard_map/ppermute | solution.py:154
  2.9 8.0 %collective-permute-start.3 = (bf16[128,512]{1,0:T(8,128)(2,1)}, bf16[128,512]{1,0:T(8,128)(2,1)S(1)}, u32[]{:S(2)}, u32[]{:S(2)}) collective-permute-start(bf16[128,512]{1,0:T(8,128)(2,1)} %refs_0_.1), channel_id=1, source_target_pairs={{0,4},{1,5},{2,6},{3,7},{4,0},{5,1},{6,2},{7,3},{8,12},{9,13},{10,... | collective-permute-start | bytes 393224 | tf_op jit(solution)/shard_map/ppermute | solution.py:154
  4.5 6.5 %collective-permute-start.5 = (bf16[128,512]{1,0:T(8,128)(2,1)}, bf16[128,512]{1,0:T(8,128)(2,1)S(1)}, u32[]{:S(2)}, u32[]{:S(2)}) collective-permute-start(bf16[128,512]{1,0:T(8,128)(2,1)} %refs_0_.1), channel_id=1, source_target_pairs={{0,6},{1,7},{2,4},{3,5},{4,2},{5,3},{6,0},{7,1},{8,14},{9,15},{10,... | collective-permute-start | bytes 393224 | tf_op jit(solution)/shard_map/ppermute | solution.py:154
  4.5 7.7 %collective-permute-start.1 = (bf16[128,512]{1,0:T(8,128)(2,1)}, bf16[128,512]{1,0:T(8,128)(2,1)S(1)}, u32[]{:S(2)}, u32[]{:S(2)}) collective-permute-start(bf16[128,512]{1,0:T(8,128)(2,1)} %refs_0_.1), channel_id=1, source_target_pairs={{0,1},{1,0},{2,3},{3,2},{4,5},{5,4},{6,7},{7,6},{8,9},{9,8},{10,11... | collective-permute-start | bytes 393224 | tf_op jit(solution)/shard_map/ppermute | solution.py:154
  7.2 5.0 %collective-permute-start.2 = (bf16[128,512]{1,0:T(8,128)(2,1)S(1)}, bf16[128,512]{1,0:T(8,128)(2,1)S(1)}, u32[]{:S(2)}, u32[]{:S(2)}) collective-permute-start(bf16[128,512]{1,0:T(8,128)(2,1)S(1)} %collective-permute-done.refs_2_), channel_id=1, source_target_pairs={{0,1},{1,0},{2,3},{3,2},{4,5},{5,4},{6,7},{7,6},{8,9},{9,8},{10,11... | collective-permute-start | bytes 393224 | tf_op jit(solution)/shard_map/ppermute | solution.py:154
  10.9 1.3 %collective-permute-start.4 = (bf16[128,512]{1,0:T(8,128)(2,1)S(1)}, bf16[128,512]{1,0:T(8,128)(2,1)S(1)}, u32[]{:S(2)}, u32[]{:S(2)}) collective-permute-start(bf16[128,512]{1,0:T(8,128)(2,1)S(1)} %collective-permute-done.3.refs_4_), channel_id=1, source_target_pairs={{0,1},{1,0},{2,3},{3,2},{4,5},{5,4},{6,7},{7,6},{8,9},{9,8},{10,11... | collective-permute-start | bytes 393224 | tf_op jit(solution)/shard_map/ppermute | solution.py:154
  10.9 1.5 %collective-permute-start.6 = (bf16[128,512]{1,0:T(8,128)(2,1)S(1)}, bf16[128,512]{1,0:T(8,128)(2,1)S(1)}, u32[]{:S(2)}, u32[]{:S(2)}) collective-permute-start(bf16[128,512]{1,0:T(8,128)(2,1)S(1)} %collective-permute-done.5.refs_6_), channel_id=1, source_target_pairs={{0,1},{1,0},{2,3},{3,2},{4,5},{5,4},{6,7},{7,6},{8,9},{9,8},{10,11... | collective-permute-start | bytes 393224 | tf_op jit(solution)/shard_map/ppermute | solution.py:154
  12.5 0.9 %copy-start = (bf16[128,512]{1,0:T(8,128)(2,1)S(1)}, bf16[128,512]{1,0:T(8,128)(2,1)}, u32[]{:S(2)}) copy-start(bf16[128,512]{1,0:T(8,128)(2,1)} %refs_0_.1) | copy-start | bytes 393220
  59.9 3.9 %collective-permute-start.7 = (f32[4,4,7,32,128]{4,3,2,1,0:T(8,128)S(1)}, f32[4,4,7,32,128]{4,3,2,1,0:T(8,128)S(1)}, u32[]{:S(2)}, u32[]{:S(2)}) collective-permute-start(f32[4,4,7,32,128]{4,3,2,1,0:T(8,128)S(1)} %get-tuple-element.12), channel_id=1, source_target_pairs={{0,1},{1,0},{2,3},{3,2},{4,5},{5,4},{6,7},{7,6},{8,9},{9,8},{10,11... | collective-permute-start | bytes 5505032 | tf_op jit(solution)/shard_map/ppermute | solution.py:154
  64.8 8.2 %collective-permute-start.11 = (s16[2,2,240,128]{3,2,1,0:T(8,128)(2,1)S(1)}, s16[2,2,240,128]{3,2,1,0:T(8,128)(2,1)S(1)}, u32[]{:S(2)}, u32[]{:S(2)}) collective-permute-start(s16[2,2,240,128]{3,2,1,0:T(8,128)(2,1)S(1)} %get-tuple-element.42), channel_id=1, source_target_pairs={{0,4},{1,5},{2,6},{3,7},{4,0},{5,1},{6,2},{7,3},{8,12},{9,13},{10,... | collective-permute-start | bytes 737288 | tf_op jit(solution)/shard_map/ppermute | solution.py:154
  66.4 7.9 %collective-permute-start.8 = (s16[2,2,240,128]{3,2,1,0:T(8,128)(2,1)S(1)}, s16[2,2,240,128]{3,2,1,0:T(8,128)(2,1)S(1)}, u32[]{:S(2)}, u32[]{:S(2)}) collective-permute-start(s16[2,2,240,128]{3,2,1,0:T(8,128)(2,1)S(1)} %get-tuple-element.43), channel_id=1, source_target_pairs={{0,2},{1,3},{2,0},{3,1},{4,6},{5,7},{6,4},{7,5},{8,10},{9,11},{10,... | collective-permute-start | bytes 737288 | tf_op jit(solution)/shard_map/ppermute | solution.py:154
  74.7 4.9 %collective-permute-start.9 = (s16[2,240,128]{2,1,0:T(8,128)(2,1)S(1)}, s16[2,240,128]{2,1,0:T(8,128)(2,1)S(1)}, u32[]{:S(2)}, u32[]{:S(2)}) collective-permute-start(s16[2,240,128]{2,1,0:T(8,128)(2,1)S(1)} %get-tuple-element.41), channel_id=1, source_target_pairs={{0,4},{1,5},{2,6},{3,7},{4,0},{5,1},{6,2},{7,3},{8,12},{9,13},{10,... | collective-permute-start | bytes 368648 | tf_op jit(solution)/shard_map/ppermute | solution.py:154
  75.3 4.9 %collective-permute-start.12 = (s16[2,240,128]{2,1,0:T(8,128)(2,1)S(1)}, s16[2,240,128]{2,1,0:T(8,128)(2,1)S(1)}, u32[]{:S(2)}, u32[]{:S(2)}) collective-permute-start(s16[2,240,128]{2,1,0:T(8,128)(2,1)S(1)} %get-tuple-element.40), channel_id=1, source_target_pairs={{0,2},{1,3},{2,0},{3,1},{4,6},{5,7},{6,4},{7,5},{8,10},{9,11},{10,... | collective-permute-start | bytes 368648 | tf_op jit(solution)/shard_map/ppermute | solution.py:154
  80.5 6.2 %collective-permute-start.14 = (s16[1,240,128]{2,1,0:T(8,128)(2,1)S(1)}, s16[1,240,128]{2,1,0:T(8,128)(2,1)S(1)}, u32[]{:S(2)}, u32[]{:S(2)}) collective-permute-start(s16[1,240,128]{2,1,0:T(8,128)(2,1)S(1)} %get-tuple-element.39), channel_id=1, source_target_pairs={{0,24},{8,16},{16,8},{24,0},{1,25},{9,17},{17,9},{25,1},{2,26},{10... | collective-permute-start | bytes 184328 | tf_op jit(solution)/shard_map/ppermute | solution.py:154
  84.2 5.1 %collective-permute-start.13 = (s16[1,240,128]{2,1,0:T(8,128)(2,1)S(1)}, s16[1,240,128]{2,1,0:T(8,128)(2,1)S(1)}, u32[]{:S(2)}, u32[]{:S(2)}) collective-permute-start(s16[1,240,128]{2,1,0:T(8,128)(2,1)S(1)} %get-tuple-element.38), channel_id=1, source_target_pairs={{0,16},{8,24},{16,0},{24,8},{1,17},{9,25},{17,1},{25,9},{2,18},{10... | collective-permute-start | bytes 184328 | tf_op jit(solution)/shard_map/ppermute | solution.py:154
  84.2 5.2 %collective-permute-start.10 = (s16[1,240,128]{2,1,0:T(8,128)(2,1)S(1)}, s16[1,240,128]{2,1,0:T(8,128)(2,1)S(1)}, u32[]{:S(2)}, u32[]{:S(2)}) collective-permute-start(s16[1,240,128]{2,1,0:T(8,128)(2,1)S(1)} %get-tuple-element.37), channel_id=1, source_target_pairs={{0,8},{8,0},{16,24},{24,16},{1,9},{9,1},{17,25},{25,17},{2,10},{10... | collective-permute-start | bytes 184328 | tf_op jit(solution)/shard_map/ppermute | solution.py:154

commit v6 on v5

--- a/solution.py
+++ b/solution.py
@@ -9,7 +9,7 @@
 from jax.sharding import PartitionSpec as P
 
 
-def band_kernel(sizes, lists_ref, *refs):
+def band_kernel(sizes, slot_lists_ref, *refs):
     aux_blocks, span, depth, edge, width, slots, groups = sizes
     coeff_refs, refs = refs[:slots], refs[slots:]
     integrals_ref, keep_ref, send_ref = refs[:3]
@@ -36,7 +36,7 @@
             for m in range(span):
                 load(block + 1, m).start()
 
-        listed = [lists_ref[block, j] for j in range(span)]
+        listed = [slot_lists_ref[block, j] ^ orb for j in range(span)]
         for n in range(span):
             chosen[n * edge : (n + 1) * edge, :] = coeffs[listed[n] ^ orb]
         for m in range(span):
@@ -85,7 +85,7 @@
                 ref[s, g ^ aux] = band[2 * s + side, :, g * rows : (g + 1) * rows]
 
 
-def band_partials(block_lists, coeff_slots, three_centre, groups):
+def band_partials(slot_lists, coeff_slots, three_centre, groups):
     aux_blocks, span, _, depth, edge, _ = three_centre.shape
     width = coeff_slots[0].shape[1]
     slots = len(coeff_slots)
@@ -117,7 +117,7 @@
         ],
         compiler_params=pltpu.CompilerParams(vmem_limit_bytes=held + given + 4 * 2**20),
         name="band_partials",
-    )(block_lists, *coeff_slots, three_centre)
+    )(slot_lists, *coeff_slots, three_centre)
 
 
 LEVELS = 32767
@@ -156,13 +156,14 @@
     def swap_sums(value, axis, bits):
         return decode(swap(encode(value), axis, bits), *value.shape[-3:-1])
 
-    slots = {0: occupied, 1: swap(occupied, "orb", 1)}
+    slots = {1: swap(occupied, "orb", 1)}
+    slots[0] = swap(slots[1], "orb", 1)
     for s in range(2, orb_size, 2):
         slots[s] = swap(occupied, "orb", s)
-    slots[2], block_lists = lax.optimization_barrier((slots[2], block_lists + 0))
+    slots[2], slot_lists = lax.optimization_barrier((slots[2], block_lists ^ lax.axis_index("orb")))
     for s in range(2, orb_size, 2):
         slots[s + 1] = swap(slots[s], "orb", 1)
-    keep, send = band_partials(block_lists, [slots[s] for s in range(orb_size)], three_centre, aux_size)
+    keep, send = band_partials(slot_lists, [slots[s] for s in range(orb_size)], three_centre, aux_size)
 
     summed = keep + swap(send, "orb", 1)
     bits = list(range(1, orb_size.bit_length() - 1))

time: 90.2 us -> 90.3 us (level)
  local copies, waits for them, and re-layouts: 1.87 us -> 0.96 us
    ppermute x15 -> x16, waiting for transfers between devices: 25.4 us -> 26.2 us  [swap(): return lax.ppermute(value, axis, [(i, i ^ bits) for i in range(size)])]
    ppermute x15 -> x16, starting transfers between devices: 13.4 us -> 13.6 us  [swap(): return lax.ppermute(value, axis, [(i, i ^ bits) for i in range(size)])]
  transfers between devices with their start and end apart: 15 -> 16, of which waited for: 11 -> 11; matrix products, arithmetic and copies ran while one was open for 1% -> 1% of each run, Pallas kernels for 0% -> 0%
where the time goes in v6:
time: 90.3 us; the launch traced here: 90.1 us
  Pallas kernels  46.5 us (51%)
  waiting for transfers between devices  26.2 us (29%)
  starting transfers between devices  13.6 us (15%)
  other arithmetic  2.63 us (3%)
  local copies, waits for them, and re-layouts  0.96 us (1%)
    pallas_call x1, Pallas kernels, band_partials(): pl.pallas_call(functools.partial(band_kernel, sizes), out_shape=[jax.Shap...  46.5 us
    ppermute x16, waiting for transfers between devices, swap(): return lax.ppermute(value, axis, [(i, i ^ bits) for i in range(size)])  26.2 us
    ppermute x16, starting transfers between devices, swap(): return lax.ppermute(value, axis, [(i, i ^ bits) for i in range(size)])  13.6 us
  transfers between devices with their start and end apart: 16, of which 11 were waited for; matrix products, arithmetic and copies ran while one was open for 1% of the time, Pallas kernels for 0%

profile of v6, /device:TPU:0, one launch (start us, length us, event | category | flops | bytes accessed | tf_op | source)
XLA Modules:
  0.0 90.1 jit_solution(14458701169359408648)
XLA Ops:
  0.0 2.9 %collective-permute-start = (bf16[128,512]{1,0:T(8,128)(2,1)}, bf16[128,512]{1,0:T(8,128)(2,1)S(1)}, u32[]{:S(2)}, u32[]{:S(2)}) collective-permute-start(bf16[128,512]{1,0:T(8,128)(2,1)} %param.5), channel_id=1, source_target_pairs={{0,2},{1,3},{2,0},{3,1},{4,6},{5,7},{6,4},{7,5},{8,10},{9,11},{10,... | collective-permute-start | bytes 393224 | tf_op jit(solution)/shard_map/ppermute | solution.py:154
  2.9 1.5 %collective-permute-start.4 = (bf16[128,512]{1,0:T(8,128)(2,1)}, bf16[128,512]{1,0:T(8,128)(2,1)S(1)}, u32[]{:S(2)}, u32[]{:S(2)}) collective-permute-start(bf16[128,512]{1,0:T(8,128)(2,1)} %param.5), channel_id=1, source_target_pairs={{0,4},{1,5},{2,6},{3,7},{4,0},{5,1},{6,2},{7,3},{8,12},{9,13},{10,... | collective-permute-start | bytes 393224 | tf_op jit(solution)/shard_map/ppermute | solution.py:154
  4.5 0.8 copy.5
  5.2 1.4 %collective-permute-done.refs_2_ = bf16[128,512]{1,0:T(8,128)(2,1)S(1)} collective-permute-done((bf16[128,512]{1,0:T(8,128)(2,1)}, bf16[128,512]{1,0:T(8,128)(2,1)S(1)}, u32[]{:S(2)}, u32[]{:S(2)}) %collective-permute-start) | collective-permute-done | bytes 131104 | tf_op jit(solution)/shard_map/ppermute | solution.py:154
  6.7 0.5 collective-permute-start.2
  7.2 4.7 %collective-permute-done.4.refs_4_ = bf16[128,512]{1,0:T(8,128)(2,1)S(1)} collective-permute-done((bf16[128,512]{1,0:T(8,128)(2,1)}, bf16[128,512]{1,0:T(8,128)(2,1)S(1)}, u32[]{:S(2)}, u32[]{:S(2)}) %collective-permute-start.4) | collective-permute-done | bytes 131104 | tf_op jit(solution)/shard_map/ppermute | solution.py:154
  11.9 0.5 collective-permute-start.7
  12.4 0.8 collective-permute-done.5.refs_5_
  13.4 46.5 %band_partials.1 = (f32[4,4,7,32,128]{4,3,2,1,0:T(8,128)S(1)}, f32[4,4,7,32,128]{4,3,2,1,0:T(8,128)S(1)}) custom-call(s32[8,3]{1,0:T(8,128)S(1)} %broadcast_xor_fusion.slot_lists_ref, bf16[128,512]{1,0:T(8,128)(2,1)S(1)} %collective-permute-done.2.refs_0_, bf16[128,512]{1,0:T(8,128)(2,1)S(1)} %collective-permute-done.1.refs_1_, ...), custom_call_target="tpu_custom_call" | custom-call | tf_op jit(solution)/shard_map/band_partials/pallas_call | solution.py:108
  60.0 0.4 collective-permute-start.8
  60.4 3.4 %collective-permute-done.8 = f32[4,4,7,32,128]{4,3,2,1,0:T(8,128)S(1)} collective-permute-done((f32[4,4,7,32,128]{4,3,2,1,0:T(8,128)S(1)}, f32[4,4,7,32,128]{4,3,2,1,0:T(8,128)S(1)}, u32[]{:S(2)}, u32[]{:S(2)}) %collective-permute-start.8) | collective-permute-done | bytes 1835040 | tf_op jit(solution)/shard_map/ppermute | solution.py:154
  63.8 0.4 add.195
  64.8 1.6 %collective-permute-start.12 = (s16[2,2,240,128]{3,2,1,0:T(8,128)(2,1)S(1)}, s16[2,2,240,128]{3,2,1,0:T(8,128)(2,1)S(1)}, u32[]{:S(2)}, u32[]{:S(2)}) collective-permute-start(s16[2,2,240,128]{3,2,1,0:T(8,128)(2,1)S(1)} %get-tuple-element.42), channel_id=1, source_target_pairs={{0,4},{1,5},{2,6},{3,7},{4,0},{5,1},{6,2},{7,3},{8,12},{9,13},{10,... | collective-permute-start | bytes 737288 | tf_op jit(solution)/shard_map/ppermute | solution.py:154
  66.4 0.5 collective-permute-start.9
  67.0 6.1 %collective-permute-done.12 = s16[2,2,240,128]{3,2,1,0:T(8,128)(2,1)S(1)} collective-permute-done((s16[2,2,240,128]{3,2,1,0:T(8,128)(2,1)S(1)}, s16[2,2,240,128]{3,2,1,0:T(8,128)(2,1)S(1)}, u32[]{:S(2)}, u32[]{:S(2)}) %collective-permute-start.12) | collective-permute-done | bytes 245792 | tf_op jit(solution)/shard_map/ppermute | solution.py:154
  73.3 1.0 %collective-permute-done.9 = s16[2,2,240,128]{3,2,1,0:T(8,128)(2,1)S(1)} collective-permute-done((s16[2,2,240,128]{3,2,1,0:T(8,128)(2,1)S(1)}, s16[2,2,240,128]{3,2,1,0:T(8,128)(2,1)S(1)}, u32[]{:S(2)}, u32[]{:S(2)}) %collective-permute-start.9) | collective-permute-done | bytes 245792 | tf_op jit(solution)/shard_map/ppermute | solution.py:154
  74.7 0.6 collective-permute-start.10
  75.3 0.5 collective-permute-start.13
  75.9 3.8 %collective-permute-done.10 = s16[2,240,128]{2,1,0:T(8,128)(2,1)S(1)} collective-permute-done((s16[2,240,128]{2,1,0:T(8,128)(2,1)S(1)}, s16[2,240,128]{2,1,0:T(8,128)(2,1)S(1)}, u32[]{:S(2)}, u32[]{:S(2)}) %collective-permute-start.10) | collective-permute-done | bytes 122912 | tf_op jit(solution)/shard_map/ppermute | solution.py:154
  80.5 3.7 %collective-permute-start.15 = (s16[1,240,128]{2,1,0:T(8,128)(2,1)S(1)}, s16[1,240,128]{2,1,0:T(8,128)(2,1)S(1)}, u32[]{:S(2)}, u32[]{:S(2)}) collective-permute-start(s16[1,240,128]{2,1,0:T(8,128)(2,1)S(1)} %get-tuple-element.39), channel_id=1, source_target_pairs={{0,24},{8,16},{16,8},{24,0},{1,25},{9,17},{17,9},{25,1},{2,26},{10... | collective-permute-start | bytes 184328 | tf_op jit(solution)/shard_map/ppermute | solution.py:154
  84.2 0.8 collective-permute-start.11
  85.0 1.7 %collective-permute-done.15 = s16[1,240,128]{2,1,0:T(8,128)(2,1)S(1)} collective-permute-done((s16[1,240,128]{2,1,0:T(8,128)(2,1)S(1)}, s16[1,240,128]{2,1,0:T(8,128)(2,1)S(1)}, u32[]{:S(2)}, u32[]{:S(2)}) %collective-permute-start.15) | collective-permute-done | bytes 61472 | tf_op jit(solution)/shard_map/ppermute | solution.py:154
  86.7 2.6 %collective-permute-done.14 = s16[1,240,128]{2,1,0:T(8,128)(2,1)S(1)} collective-permute-done((s16[1,240,128]{2,1,0:T(8,128)(2,1)S(1)}, s16[1,240,128]{2,1,0:T(8,128)(2,1)S(1)}, u32[]{:S(2)}, u32[]{:S(2)}) %collective-permute-start.14) | collective-permute-done | bytes 61472 | tf_op jit(solution)/shard_map/ppermute | solution.py:154
  89.4 0.7 copy_bitcast_fusion
  (55 shorter events, 2.3 us)
Async XLA Ops:
  0.0 6.6 %collective-permute-start = (bf16[128,512]{1,0:T(8,128)(2,1)}, bf16[128,512]{1,0:T(8,128)(2,1)S(1)}, u32[]{:S(2)}, u32[]{:S(2)}) collective-permute-start(bf16[128,512]{1,0:T(8,128)(2,1)} %param.5), channel_id=1, source_target_pairs={{0,2},{1,3},{2,0},{3,1},{4,6},{5,7},{6,4},{7,5},{8,10},{9,11},{10,... | collective-permute-start | bytes 393224 | tf_op jit(solution)/shard_map/ppermute | solution.py:154
  2.9 3.7 %collective-permute-start.1 = (bf16[128,512]{1,0:T(8,128)(2,1)}, bf16[128,512]{1,0:T(8,128)(2,1)S(1)}, u32[]{:S(2)}, u32[]{:S(2)}) collective-permute-start(bf16[128,512]{1,0:T(8,128)(2,1)} %param.5), channel_id=1, source_target_pairs={{0,1},{1,0},{2,3},{3,2},{4,5},{5,4},{6,7},{7,6},{8,9},{9,8},{10,11... | collective-permute-start | bytes 393224 | tf_op jit(solution)/shard_map/ppermute | solution.py:154
  2.9 8.9 %collective-permute-start.4 = (bf16[128,512]{1,0:T(8,128)(2,1)}, bf16[128,512]{1,0:T(8,128)(2,1)S(1)}, u32[]{:S(2)}, u32[]{:S(2)}) collective-permute-start(bf16[128,512]{1,0:T(8,128)(2,1)} %param.5), channel_id=1, source_target_pairs={{0,4},{1,5},{2,6},{3,7},{4,0},{5,1},{6,2},{7,3},{8,12},{9,13},{10,... | collective-permute-start | bytes 393224 | tf_op jit(solution)/shard_map/ppermute | solution.py:154
  4.5 7.4 %collective-permute-start.6 = (bf16[128,512]{1,0:T(8,128)(2,1)}, bf16[128,512]{1,0:T(8,128)(2,1)S(1)}, u32[]{:S(2)}, u32[]{:S(2)}) collective-permute-start(bf16[128,512]{1,0:T(8,128)(2,1)} %param.5), channel_id=1, source_target_pairs={{0,6},{1,7},{2,4},{3,5},{4,2},{5,3},{6,0},{7,1},{8,14},{9,15},{10,... | collective-permute-start | bytes 393224 | tf_op jit(solution)/shard_map/ppermute | solution.py:154
  6.6 5.7 %collective-permute-start.3 = (bf16[128,512]{1,0:T(8,128)(2,1)S(1)}, bf16[128,512]{1,0:T(8,128)(2,1)S(1)}, u32[]{:S(2)}, u32[]{:S(2)}) collective-permute-start(bf16[128,512]{1,0:T(8,128)(2,1)S(1)} %collective-permute-done.refs_2_), channel_id=1, source_target_pairs={{0,1},{1,0},{2,3},{3,2},{4,5},{5,4},{6,7},{7,6},{8,9},{9,8},{10,11... | collective-permute-start | bytes 393224 | tf_op jit(solution)/shard_map/ppermute | solution.py:154
  6.7 5.7 %collective-permute-start.2 = (bf16[128,512]{1,0:T(8,128)(2,1)S(1)}, bf16[128,512]{1,0:T(8,128)(2,1)S(1)}, u32[]{:S(2)}, u32[]{:S(2)}) collective-permute-start(bf16[128,512]{1,0:T(8,128)(2,1)S(1)} %collective-permute-done.1.refs_1_), channel_id=1, source_target_pairs={{0,1},{1,0},{2,3},{3,2},{4,5},{5,4},{6,7},{7,6},{8,9},{9,8},{10,11... | collective-permute-start | bytes 393224 | tf_op jit(solution)/shard_map/ppermute | solution.py:154
  11.9 1.3 %collective-permute-start.5 = (bf16[128,512]{1,0:T(8,128)(2,1)S(1)}, bf16[128,512]{1,0:T(8,128)(2,1)S(1)}, u32[]{:S(2)}, u32[]{:S(2)}) collective-permute-start(bf16[128,512]{1,0:T(8,128)(2,1)S(1)} %collective-permute-done.4.refs_4_), channel_id=1, source_target_pairs={{0,1},{1,0},{2,3},{3,2},{4,5},{5,4},{6,7},{7,6},{8,9},{9,8},{10,11... | collective-permute-start | bytes 393224 | tf_op jit(solution)/shard_map/ppermute | solution.py:154
  11.9 1.5 %collective-permute-start.7 = (bf16[128,512]{1,0:T(8,128)(2,1)S(1)}, bf16[128,512]{1,0:T(8,128)(2,1)S(1)}, u32[]{:S(2)}, u32[]{:S(2)}) collective-permute-start(bf16[128,512]{1,0:T(8,128)(2,1)S(1)} %collective-permute-done.6.refs_6_), channel_id=1, source_target_pairs={{0,1},{1,0},{2,3},{3,2},{4,5},{5,4},{6,7},{7,6},{8,9},{9,8},{10,11... | collective-permute-start | bytes 393224 | tf_op jit(solution)/shard_map/ppermute | solution.py:154
  60.0 3.9 %collective-permute-start.8 = (f32[4,4,7,32,128]{4,3,2,1,0:T(8,128)S(1)}, f32[4,4,7,32,128]{4,3,2,1,0:T(8,128)S(1)}, u32[]{:S(2)}, u32[]{:S(2)}) collective-permute-start(f32[4,4,7,32,128]{4,3,2,1,0:T(8,128)S(1)} %get-tuple-element.12), channel_id=1, source_target_pairs={{0,1},{1,0},{2,3},{3,2},{4,5},{5,4},{6,7},{7,6},{8,9},{9,8},{10,11... | collective-permute-start | bytes 5505032 | tf_op jit(solution)/shard_map/ppermute | solution.py:154
  64.8 8.2 %collective-permute-start.12 = (s16[2,2,240,128]{3,2,1,0:T(8,128)(2,1)S(1)}, s16[2,2,240,128]{3,2,1,0:T(8,128)(2,1)S(1)}, u32[]{:S(2)}, u32[]{:S(2)}) collective-permute-start(s16[2,2,240,128]{3,2,1,0:T(8,128)(2,1)S(1)} %get-tuple-element.42), channel_id=1, source_target_pairs={{0,4},{1,5},{2,6},{3,7},{4,0},{5,1},{6,2},{7,3},{8,12},{9,13},{10,... | collective-permute-start | bytes 737288 | tf_op jit(solution)/shard_map/ppermute | solution.py:154
  66.4 7.9 %collective-permute-start.9 = (s16[2,2,240,128]{3,2,1,0:T(8,128)(2,1)S(1)}, s16[2,2,240,128]{3,2,1,0:T(8,128)(2,1)S(1)}, u32[]{:S(2)}, u32[]{:S(2)}) collective-permute-start(s16[2,2,240,128]{3,2,1,0:T(8,128)(2,1)S(1)} %get-tuple-element.43), channel_id=1, source_target_pairs={{0,2},{1,3},{2,0},{3,1},{4,6},{5,7},{6,4},{7,5},{8,10},{9,11},{10,... | collective-permute-start | bytes 737288 | tf_op jit(solution)/shard_map/ppermute | solution.py:154
  74.7 4.9 %collective-permute-start.10 = (s16[2,240,128]{2,1,0:T(8,128)(2,1)S(1)}, s16[2,240,128]{2,1,0:T(8,128)(2,1)S(1)}, u32[]{:S(2)}, u32[]{:S(2)}) collective-permute-start(s16[2,240,128]{2,1,0:T(8,128)(2,1)S(1)} %get-tuple-element.41), channel_id=1, source_target_pairs={{0,4},{1,5},{2,6},{3,7},{4,0},{5,1},{6,2},{7,3},{8,12},{9,13},{10,... | collective-permute-start | bytes 368648 | tf_op jit(solution)/shard_map/ppermute | solution.py:154
  75.3 4.9 %collective-permute-start.13 = (s16[2,240,128]{2,1,0:T(8,128)(2,1)S(1)}, s16[2,240,128]{2,1,0:T(8,128)(2,1)S(1)}, u32[]{:S(2)}, u32[]{:S(2)}) collective-permute-start(s16[2,240,128]{2,1,0:T(8,128)(2,1)S(1)} %get-tuple-element.40), channel_id=1, source_target_pairs={{0,2},{1,3},{2,0},{3,1},{4,6},{5,7},{6,4},{7,5},{8,10},{9,11},{10,... | collective-permute-start | bytes 368648 | tf_op jit(solution)/shard_map/ppermute | solution.py:154
  80.5 6.2 %collective-permute-start.15 = (s16[1,240,128]{2,1,0:T(8,128)(2,1)S(1)}, s16[1,240,128]{2,1,0:T(8,128)(2,1)S(1)}, u32[]{:S(2)}, u32[]{:S(2)}) collective-permute-start(s16[1,240,128]{2,1,0:T(8,128)(2,1)S(1)} %get-tuple-element.39), channel_id=1, source_target_pairs={{0,24},{8,16},{16,8},{24,0},{1,25},{9,17},{17,9},{25,1},{2,26},{10... | collective-permute-start | bytes 184328 | tf_op jit(solution)/shard_map/ppermute | solution.py:154
  84.2 5.1 %collective-permute-start.14 = (s16[1,240,128]{2,1,0:T(8,128)(2,1)S(1)}, s16[1,240,128]{2,1,0:T(8,128)(2,1)S(1)}, u32[]{:S(2)}, u32[]{:S(2)}) collective-permute-start(s16[1,240,128]{2,1,0:T(8,128)(2,1)S(1)} %get-tuple-element.38), channel_id=1, source_target_pairs={{0,16},{8,24},{16,0},{24,8},{1,17},{9,25},{17,1},{25,9},{2,18},{10... | collective-permute-start | bytes 184328 | tf_op jit(solution)/shard_map/ppermute | solution.py:154
  84.2 5.2 %collective-permute-start.11 = (s16[1,240,128]{2,1,0:T(8,128)(2,1)S(1)}, s16[1,240,128]{2,1,0:T(8,128)(2,1)S(1)}, u32[]{:S(2)}, u32[]{:S(2)}) collective-permute-start(s16[1,240,128]{2,1,0:T(8,128)(2,1)S(1)} %get-tuple-element.37), channel_id=1, source_target_pairs={{0,8},{8,0},{16,24},{24,16},{1,9},{9,1},{17,25},{25,17},{2,10},{10... | collective-permute-start | bytes 184328 | tf_op jit(solution)/shard_map/ppermute | solution.py:154
